TPU v7x, 1024 devices: a whole 8x8x8 slice. The times are simulated.
1024 devices in a mesh: dp: 64 (over y, z), expert: 16 (over x, core).
Axes of the slice: x: 8, y: 8, z: 8, core: 2. Of those that a mesh axis runs over, the one named last changes fastest.
Arguments:
- tokens: bfloat16 [16, 128, 7168], P('expert', 'dp'), may hold values from -6 to 6
- slot_grads: bfloat16 [16, 128, 8, 2048], P('expert', 'dp'), may hold values from -0.796875 to 0.796875
- expert_ids: int32 [16, 128, 8], P('expert'), may hold values from 0 to 31, all different within a row; in each aligned block of 128 rows (0 to 127, 128 to 255, ..., all dimensions but the last counted through in order) at most 48 rows name the same one
Outputs:
- weight_grad: bfloat16 [32, 64, 896, 256], P('expert', 'dp')
Inputs may be any that keep to these rules, and one draw needn't show every extreme that they name: `expert_ids`: each token names 8 different experts. Among the 128 tokens of one group, no expert is named by more than 48 tokens, a bound that some block reaches.
All inputs are finite; a program needn't handle non-finite values.
Results may differ from a plain program's by a relative error of at most 0.001.
Values may be sent and summed in bfloat16 or wider, within the bound.
No kernel may reach another device: no remote copies, remote signals or barrier semaphores. Data moves between devices by JAX's collectives and lax.ppermute only.
A program may use at most 128 MiB of HBM per device.

v0:
```python
import jax
import jax.numpy as jnp
from jax import lax
from jax.sharding import PartitionSpec as P

EXP_DEV = 2
DB = 8


def slot_buffers(rows_x, rows_g, group_ids, expert_count, capacity, top_count):
    flat_ids = group_ids.reshape(-1)
    hits = (flat_ids[:, None] == jnp.arange(expert_count, dtype=jnp.int32)[None, :]).astype(
        jnp.int32
    )
    ranks = jnp.sum((jnp.cumsum(hits, axis=0) - hits) * hits, axis=1)
    target = flat_ids * capacity + ranks
    source = (
        jnp.zeros((expert_count * capacity,), jnp.int32)
        .at[target]
        .set(jnp.arange(flat_ids.shape[0], dtype=jnp.int32) + 1)
    )
    filled = source > 0
    slot_index = jnp.maximum(source - 1, 0)
    left = jnp.where(filled[:, None], rows_x[slot_index // top_count], jnp.zeros((), rows_x.dtype))
    right = jnp.where(
        filled[:, None],
        rows_g.reshape(-1, rows_g.shape[-1])[slot_index],
        jnp.zeros((), rows_g.dtype),
    )
    return (left, right)


def expert_blocks(pair):
    left, right = pair
    return jnp.einsum("sicd,sicf->idf", left, right, preferred_element_type=jnp.float32).astype(
        jnp.bfloat16
    )


def body(tokens, slot_grads, expert_ids):
    dp_count = lax.axis_size("dp")
    owner_count = lax.axis_size("expert")
    col_blocks = dp_count // DB
    block_rows = tokens.shape[2] // DB
    block_cols = slot_grads.shape[3] // col_blocks
    local_tokens = tokens.shape[1]
    top_count = slot_grads.shape[2]
    x_parts = tokens[0].reshape(local_tokens, DB, block_rows).transpose(1, 0, 2)
    x_send = jnp.broadcast_to(x_parts[:, None], (DB, col_blocks, local_tokens, block_rows)).reshape(
        dp_count, local_tokens, block_rows
    )
    g_parts = (
        slot_grads[0].reshape(local_tokens, top_count, col_blocks, block_cols).transpose(2, 0, 1, 3)
    )
    g_send = jnp.broadcast_to(
        g_parts[None], (DB, col_blocks, local_tokens, top_count, block_cols)
    ).reshape(dp_count, local_tokens, top_count, block_cols)
    x_got, g_got = (
        lax.all_to_all(x_send, "dp", split_axis=0, concat_axis=0, tiled=True),
        lax.all_to_all(g_send, "dp", split_axis=0, concat_axis=0, tiled=True),
    )
    rows_x = x_got.reshape(dp_count * local_tokens, block_rows)
    rows_g = g_got.reshape(dp_count * local_tokens, top_count, block_cols)
    group_tokens = rows_x.shape[0]
    expert_count = EXP_DEV * owner_count
    capacity = max(2, min(group_tokens, group_tokens * top_count * 3 // (2 * expert_count)))
    left, right = slot_buffers(rows_x, rows_g, expert_ids[0], expert_count, capacity, top_count)
    left = left.reshape(owner_count, EXP_DEV, capacity, block_rows)
    right = right.reshape(owner_count, EXP_DEV, capacity, block_cols)
    grads = expert_blocks(
        (
            lax.all_to_all(left, "expert", split_axis=0, concat_axis=0, tiled=True),
            lax.all_to_all(right, "expert", split_axis=0, concat_axis=0, tiled=True),
        )
    )
    return grads[:, None]


def solution(mesh):
    placed = (P("expert", "dp", None), P("expert", "dp", None, None), P("expert", None, None))
    return jax.shard_map(
        body, mesh=mesh, in_specs=placed, out_specs=P("expert", "dp", None, None), check_vma=False
    )
```

profile of v0, /device:TPU:1, one launch (start us, length us, event | category | flops | bytes accessed | tf_op | source)
XLA Modules:
  0.0 170.1 jit_solution(11382467227348683777)
XLA Ops:
  0.0 0.0 copy-start.1
  0.0 0.0 copy-start
  0.0 0.9 copy.25
  0.9 0.8 broadcast_in_dim.57
  1.7 24.0 %all-to-all-start.2 = ((bf16[64,2,8,256]{3,2,1,0:T(8,128)(2,1)}), bf16[64,2,8,256]{3,2,1,0:T(8,128)(2,1)S(1)}, u32[]{:S(2)}, u32[]{:S(2)}) async-start(bf16[64,2,8,256]{3,2,1,0:T(8,128)(2,1)} %bitcast.9), calls=%async_computation.2 | async-start | bytes 1048576 | tf_op jit(solution)/shard_map/all_to_all | solution.py:60
  25.7 0.8 copy.20
  26.5 0.1 eq.29
  26.5 0.1 eq.25
  26.7 9.0 %reduce-window.6 = s32[32,8,128]{2,1,0:T(8,128)S(1)} reduce-window(s32[32,8,128]{2,1,0:T(8,128)S(1)} %fusion.4, s32[]{:T(128)} %constant.29.clone.1), window={size=1x1x128 pad=0_0x0_0x127_0}, to_apply=%region_0.0 | reduce-window | flops 4161536 | bytes 262148 | tf_op jit(solution)/shard_map/reduce-window
  35.7 0.1 slice.12
  35.8 0.1 copy.22
  35.9 0.1 copy.23
  36.0 0.0 copy-done.1
  36.0 0.1 copy.19
  36.1 0.1 mul.21
  36.2 0.0 copy-done
  36.3 0.1 broadcast_add_fusion
  36.5 4.3 %scatter_custom_fusion = s32[1536]{0:T(1024)S(1)} fusion(s32[1024]{0:T(1024)S(1)} %bitcast.55, s32[1024]{0:T(1024)S(1)} %iota_add_fusion, s32[]{:T(128)} %constant.29.clone.1), kind=kCustom, calls=%fused_computation.27 | custom fusion | bytes 6148 | tf_op jit(solution)/shard_map/scatter | solution.py:20
  40.8 1.2 all-to-all-done.2
  42.0 0.8 broadcast_in_dim.53
  42.8 10.9 %all-to-all-start = ((bf16[64,2,896]{2,1,0:T(2,128)(2,1)}), bf16[64,2,896]{2,1,0:T(2,128)(2,1)S(1)}, u32[]{:S(2)}, u32[]{:S(2)}) async-start(bf16[64,2,896]{2,1,0:T(2,128)(2,1)} %bitcast.5), calls=%async_computation | async-start | bytes 458752 | tf_op jit(solution)/shard_map/all_to_all | solution.py:59
  53.8 0.1 broadcast_in_dim.51
  53.9 4.8 %gather_fusion.1 = bf16[1536,256]{1,0:T(8,128)(2,1)S(1)} fusion(bf16[1024,256]{1,0:T(8,128)(2,1)S(1)} %bitcast.46, s32[2048]{0:T(1024)S(1)} %pad_clamp_fusion), kind=kCustom, calls=%fused_computation.1 | custom fusion | bytes 1579008 | tf_op jit(solution)/shard_map/gather | solution.py:27
  58.7 1.2 broadcast_select_fusion.1
  59.8 6.0 %all-to-all-done = bf16[64,2,896]{2,1,0:T(2,128)(2,1)S(1)} async-done(((bf16[64,2,896]{2,1,0:T(2,128)(2,1)}), bf16[64,2,896]{2,1,0:T(2,128)(2,1)S(1)}, u32[]{:S(2)}, u32[]{:S(2)}) %all-to-all-start) | async-done | bytes 229408 | tf_op jit(solution)/shard_map/all_to_all | solution.py:59
  65.8 10.1 %all-to-all-start.3 = ((bf16[16,2,48,256]{3,2,1,0:T(8,128)(2,1)}), bf16[16,2,48,256]{3,2,1,0:T(8,128)(2,1)}, u32[]{:S(2)}, u32[]{:S(2)}) async-start(bf16[16,2,48,256]{3,2,1,0:T(8,128)(2,1)} %broadcast_select_fusion.1), calls=%async_computation.3 | async-start | bytes 1572864 | tf_op jit(solution)/shard_map/all_to_all | solution.py:73
  75.9 0.1 reshape.72
  76.0 5.7 %gather_fusion = bf16[1536,896]{1,0:T(8,128)(2,1)} fusion(bf16[128,896]{1,0:T(8,128)(2,1)S(1)} %reshape.72, s32[2048]{0:T(1024)S(1)} %pad_clamp_fusion.1), kind=kCustom, calls=%fused_computation | custom fusion | bytes 5511168 | tf_op jit(solution)/shard_map/gather | solution.py:24
  81.8 2.2 %broadcast_select_fusion = bf16[16,2,48,896]{3,2,1,0:T(8,128)(2,1)S(1)} fusion(bf16[16,2,48,896]{3,2,1,0:T(8,128)(2,1)} %bitcast.47, pred[16,2,48]{2,1,0:T(4,128)(4,1)S(1)} %broadcast_in_dim.51), kind=kLoop, calls=%fused_computation.3 | loop fusion | flops 1376256 | bytes 5506560 | tf_op jit(solution)/shard_map/jit(_where)/select_n | solution.py:24
  83.9 14.7 %all-to-all-done.3 = bf16[16,2,48,256]{3,2,1,0:T(8,128)(2,1)} async-done(((bf16[16,2,48,256]{3,2,1,0:T(8,128)(2,1)}), bf16[16,2,48,256]{3,2,1,0:T(8,128)(2,1)}, u32[]{:S(2)}, u32[]{:S(2)}) %all-to-all-start.3) | async-done | bytes 786464 | tf_op jit(solution)/shard_map/all_to_all | solution.py:73
  98.7 68.1 %all_to_all.20 = bf16[16,2,48,896]{3,2,1,0:T(8,128)(2,1)S(1)} all-to-all(bf16[16,2,48,896]{3,2,1,0:T(8,128)(2,1)S(1)} %broadcast_select_fusion), channel_id=1, replica_groups=mesh['dp'=64,'expert'=16] {'expert'}, dimensions={0} | all-to-all | bytes 5505024 | tf_op jit(solution)/shard_map/all_to_all | solution.py:72
  166.8 3.3 %fusion = bf16[2,1,896,256]{3,2,1,0:T(8,128)(2,1)} fusion(bf16[16,2,48,896]{3,2,1,0:T(8,128)(2,1)S(1)} %all_to_all.20, bf16[16,2,48,256]{3,2,1,0:T(8,128)(2,1)} %all-to-all-done.3), kind=kOutput, calls=%fused_computation.5 | convolution fusion | flops 705101824 | bytes 4456448 | tf_op jit(solution)/shard_map/sicd,sicf->idf/dot_general | solution.py:35
  (13 shorter events, 0.2 us)
Async XLA Ops:
  0.0 36.0 %copy-start.1 = (s32[1,128,8]{1,2,0:T(8,128)S(1)}, s32[1,128,8]{1,2,0:T(8,128)}, u32[]{:S(2)}) copy-start(s32[1,128,8]{1,2,0:T(8,128)} %param.5) | copy-start | bytes 12292
  0.0 36.2 %copy-start = (bf16[1,2,7168]{2,1,0:T(2,128)(2,1)S(1)}, bf16[1,2,7168]{2,1,0:T(2,128)(2,1)}, u32[]{:S(2)}) copy-start(bf16[1,2,7168]{2,1,0:T(2,128)(2,1)} %param.3) | copy-start | bytes 86020
  1.7 40.3 %all-to-all-start.2 = ((bf16[64,2,8,256]{3,2,1,0:T(8,128)(2,1)}), bf16[64,2,8,256]{3,2,1,0:T(8,128)(2,1)S(1)}, u32[]{:S(2)}, u32[]{:S(2)}) async-start(bf16[64,2,8,256]{3,2,1,0:T(8,128)(2,1)} %bitcast.9), calls=%async_computation.2 | async-start | bytes 1048576 | tf_op jit(solution)/shard_map/all_to_all | solution.py:60
  42.8 23.0 %all-to-all-start = ((bf16[64,2,896]{2,1,0:T(2,128)(2,1)}), bf16[64,2,896]{2,1,0:T(2,128)(2,1)S(1)}, u32[]{:S(2)}, u32[]{:S(2)}) async-start(bf16[64,2,896]{2,1,0:T(2,128)(2,1)} %bitcast.5), calls=%async_computation | async-start | bytes 458752 | tf_op jit(solution)/shard_map/all_to_all | solution.py:59
  65.8 32.8 %all-to-all-start.3 = ((bf16[16,2,48,256]{3,2,1,0:T(8,128)(2,1)}), bf16[16,2,48,256]{3,2,1,0:T(8,128)(2,1)}, u32[]{:S(2)}, u32[]{:S(2)}) async-start(bf16[16,2,48,256]{3,2,1,0:T(8,128)(2,1)} %broadcast_select_fusion.1), calls=%async_computation.3 | async-start | bytes 1572864 | tf_op jit(solution)/shard_map/all_to_all | solution.py:73
where the time goes:
time: 171 us; the launch traced here: 170 us
  blocking collectives  68.1 us (40%)
  starting transfers between devices  45 us (26%)
  waiting for transfers between devices  22 us (13%)
  local copies, waits for them, and re-layouts  19 us (11%)
  other arithmetic  12.6 us (7%)
  matrix products  3.29 us (2%)
    all_to_all x1, blocking collectives, body(): lax.all_to_all(left, 'expert', split_axis=0, concat_axis=0, tiled=True)  68.1 us
    all_to_all x1, starting transfers between devices, body(): lax.all_to_all(g_send, 'dp', split_axis=0, concat_axis=0, tiled=True)  24 us
    all_to_all x1, waiting for transfers between devices, body(): lax.all_to_all(right, 'expert', split_axis=0, concat_axis=0, tiled=True)  14.7 us
    all_to_all x1, starting transfers between devices, body(): lax.all_to_all(x_send, 'dp', split_axis=0, concat_axis=0, tiled=True)  10.9 us
    all_to_all x1, starting transfers between devices, body(): lax.all_to_all(right, 'expert', split_axis=0, concat_axis=0, tiled=True)  10.1 us
    another operation x3, other arithmetic  9.14 us
    all_to_all x1, waiting for transfers between devices, body(): lax.all_to_all(x_send, 'dp', split_axis=0, concat_axis=0, tiled=True)  6.04 us
    gather x1, local copies, waits for them, and re-layouts, slot_buffers(): rows_x[slot_index // top_count]  5.73 us
  transfers between devices with their start and end apart: 3, of which 3 were waited for; matrix products, arithmetic and copies ran while one was open for 17% of the time, Pallas kernels for 0%

commit v1 on v0

v1 whole, which is shorter than its diff:
```python
import functools

import jax
import jax.numpy as jnp
from jax import lax
from jax.experimental import pallas as pl
from jax.experimental.pallas import tpu as pltpu
from jax.sharding import Mesh, PartitionSpec as P

DB = 8
FB = 8
TOP = 8
TOK = 128
DBLK = 896
FBLK = 256
PIECE = FBLK // DB
EXPERTS = 32
CAP = 48
OWN = 2
OWNERS = 16
HALF = CAP // 2
LANES = 128
XROWS = DBLK + 16
STEP_ROWS = 224


def earlier():
    row = lax.broadcasted_iota(jnp.int32, (TOK, TOK), 0)
    col = lax.broadcasted_iota(jnp.int32, (TOK, TOK), 1)
    return (row < col).astype(jnp.bfloat16)


def place_kernel(ids_ref, onehot_ref):
    expert = lax.broadcasted_iota(jnp.int32, (EXPERTS, TOK), 0)
    named = jnp.zeros((EXPERTS, TOK), jnp.float32)
    for k in range(TOP):
        named += (ids_ref[k : k + 1, :] == expert).astype(jnp.float32)
    before = jnp.dot(named.astype(jnp.bfloat16), earlier(), preferred_element_type=jnp.float32)
    place = before.astype(jnp.int32) + CAP * expert
    row = lax.broadcasted_iota(jnp.int32, (OWNERS * HALF, TOK), 0)
    owner = row // HALF
    base = owner * (OWN * CAP) + (row - owner * HALF)
    for k in range(TOP):
        target = jnp.sum(
            jnp.where(ids_ref[k : k + 1, :] == expert, place, 0), axis=0, keepdims=True
        )
        for j in range(4):
            at = (j * TOP + k) * TOK
            onehot_ref[:, at : at + TOK] = (base + j * HALF == target).astype(jnp.bfloat16)


def route_kernel(pieces_ref, onehot_ref, out_ref):
    pieces = pieces_ref[...].astype(jnp.float32)
    block = lax.broadcasted_iota(jnp.int32, (TOK, LANES), 1) // PIECE
    rows = []
    for j in range(4):
        for k in range(TOP):
            half = pieces[:, (k // 4) * LANES : (k // 4 + 1) * LANES]
            shift = ((j - k) % 4) * PIECE
            moved = pltpu.roll(half, shift, 1) if shift else half
            rows.append(jnp.where(block == j, moved, 0.0).astype(jnp.bfloat16))
    out_ref[...] = jnp.dot(
        onehot_ref[...], jnp.concatenate(rows, axis=0), preferred_element_type=jnp.float32
    ).astype(jnp.bfloat16)


def spread_kernel(slots_ref, out_ref):
    source = lax.broadcasted_iota(jnp.int32, (DB * LANES, FBLK), 0)
    column = lax.broadcasted_iota(jnp.int32, (DB * LANES, FBLK), 1)
    slots = jnp.concatenate([slots_ref[y] for y in range(DB)], axis=1)
    wanted = (column // PIECE) * LANES + column % PIECE
    for j in range(4):
        pick = (source == wanted + j * PIECE).astype(jnp.bfloat16)
        out_ref[j] = jnp.dot(slots, pick, preferred_element_type=jnp.float32).astype(jnp.bfloat16)


def product_kernel(first_ref, x_ref, ids_ref, slots_ref, out_ref, dense_ref):
    @pl.when(pl.program_id(0) == 0)
    def _():
        named = []
        for e in range(OWN):
            for g in range(OWNERS):
                hit = (ids_ref[g, 0:TOP, :].astype(jnp.int32) == first_ref[0] + e).astype(jnp.float32)
                named.append(jnp.sum(hit, axis=0, keepdims=True))
        named = jnp.concatenate(named, axis=0)
        before = jnp.dot(named.astype(jnp.bfloat16), earlier(), preferred_element_type=jnp.float32)
        place = jnp.where(named > 0.0, before, -1.0).T
        number = lax.broadcasted_iota(jnp.int32, (TOK, CAP), 1).astype(jnp.float32)
        for e in range(OWN):
            for g in range(OWNERS):
                at = e * OWNERS + g
                pick = (place[:, at : at + 1] == number).astype(jnp.bfloat16)
                dense_ref[g * TOK : (g + 1) * TOK, e * FBLK : (e + 1) * FBLK] = jnp.dot(
                    pick, slots_ref[e, g], preferred_element_type=jnp.float32
                ).astype(jnp.bfloat16)

    left = jnp.concatenate([x_ref[g] for g in range(OWNERS)], axis=1)
    total = jnp.dot(left, dense_ref[...], preferred_element_type=jnp.float32)
    for e in range(OWN):
        out_ref[e] = total[:, e * FBLK : (e + 1) * FBLK].astype(jnp.bfloat16)


def params(mib):
    return pltpu.CompilerParams(vmem_limit_bytes=mib << 20)


def body(tokens, slot_grads, expert_ids):
    ids = expert_ids[0].T
    onehot = pl.pallas_call(
        place_kernel,
        out_shape=jax.ShapeDtypeStruct((OWNERS * HALF, 4 * TOP * TOK), jnp.bfloat16),
        compiler_params=params(16),
    )(ids)

    x_part = tokens[0].reshape(2, DB, DBLK).transpose(1, 0, 2)
    x_part = jnp.broadcast_to(x_part[:, None], (DB, FB, 2, DBLK))
    g_part = slot_grads[0].reshape(2, TOP, FB, DB, PIECE).transpose(3, 2, 0, 1, 4)
    g_part = g_part.reshape(DB, FB, 2, TOP * PIECE)
    send = jnp.concatenate([x_part, g_part], axis=3).reshape(DB * FB, 2, DBLK + FBLK)
    got = lax.all_to_all(send, ("y", "z"), split_axis=0, concat_axis=0, tiled=True)
    got = got.reshape(TOK, DBLK + FBLK)

    id_rows = jnp.concatenate([ids, jnp.zeros((8, TOK), jnp.int32)], axis=0)
    left = jnp.concatenate([got[:, :DBLK].T, id_rows.astype(jnp.bfloat16)], axis=0)
    left = lax.all_gather(left, ("x", "core"))

    routed = pl.pallas_call(
        route_kernel,
        out_shape=jax.ShapeDtypeStruct((OWNERS * HALF, LANES), jnp.bfloat16),
        compiler_params=params(32),
    )(got[:, DBLK:], onehot)
    routed = lax.all_to_all(
        routed.reshape(OWNERS, HALF, LANES), ("x", "core"), split_axis=0, concat_axis=0, tiled=True
    )
    slots = lax.all_to_all(
        jnp.broadcast_to(routed[None], (DB, OWNERS, HALF, LANES)),
        "y",
        split_axis=0,
        concat_axis=0,
        tiled=True,
    )
    spread = pl.pallas_call(
        spread_kernel,
        out_shape=jax.ShapeDtypeStruct((4, OWNERS * HALF, FBLK), jnp.bfloat16),
        compiler_params=params(32),
    )(slots.reshape(DB, OWNERS * HALF, LANES))
    spread = spread.reshape(OWN, 2, OWNERS, HALF, FBLK).transpose(0, 2, 1, 3, 4)
    spread = spread.reshape(OWN, OWNERS, CAP, FBLK)

    first = (OWN * lax.axis_index(("x", "core"))).astype(jnp.int32).reshape(1)
    out = pl.pallas_call(
        product_kernel,
        grid=(DBLK // STEP_ROWS,),
        in_specs=[
            pl.BlockSpec(memory_space=pltpu.SMEM),
            pl.BlockSpec((OWNERS, STEP_ROWS, TOK), lambda i: (0, i, 0)),
            pl.BlockSpec((OWNERS, 16, TOK), lambda i: (0, DBLK // 16, 0)),
            pl.BlockSpec((OWN, OWNERS, CAP, FBLK), lambda i: (0, 0, 0, 0)),
        ],
        out_specs=pl.BlockSpec((OWN, STEP_ROWS, FBLK), lambda i: (0, i, 0)),
        out_shape=jax.ShapeDtypeStruct((OWN, DBLK, FBLK), jnp.bfloat16),
        scratch_shapes=[pltpu.VMEM((OWNERS * TOK, OWN * FBLK), jnp.bfloat16)],
        compiler_params=params(32),
    )(first, left, left, spread)
    return out[:, None]


def solution(mesh):
    grid = Mesh(mesh.devices.reshape(DB, FB, 8, 2), ("y", "z", "x", "core"))
    owner, block = ("x", "core"), ("y", "z")
    placed = (P(owner, block, None), P(owner, block, None, None), P(owner, None, None))
    return jax.shard_map(
        body, mesh=grid, in_specs=placed, out_specs=P(owner, block, None, None), check_vma=False
    )
```

time: 171 us -> 114 us (0.67)
  blocking collectives: 68.1 us -> 19.3 us
  starting transfers between devices: 45 us -> 27.6 us
  waiting for transfers between devices: 22 us -> 35.9 us
  between operations: 0.17 us -> 13.5 us
  local copies, waits for them, and re-layouts: 19 us -> 7.2 us
  other arithmetic: 12.6 us -> 1.01 us
  Pallas kernels: 0 us -> 9.03 us
  matrix products: 3.29 us -> 0 us
    all_to_all x1, blocking collectives: 68.1 us -> 19.3 us  [body(): lax.all_to_all(routed.reshape(OWNERS, HALF, LANES), ('x', 'core'), split_...]
    all_to_all x3 -> x2, starting transfers between devices: 45 us -> 27.5 us  [the longest x1 24 us: body(): lax.all_to_all(send, ('y', 'z'), split_axis=0, concat_axis=0, tiled=True)]
    all_to_all x3 -> x2, waiting for transfers between devices: 22 us -> 35.9 us  [the longest x1 23.6 us: body(): lax.all_to_all(jnp.broadcast_to(routed[None], (DB, OWNERS, HALF, LANES)),...]
    gather x2 -> x0, local copies, waits for them, and re-layouts: 10.5 us -> none  [the longest x1 5.73 us: slot_buffers(): rows_x[slot_index // top_count]]
    another operation x3 -> x1, other arithmetic: 9.14 us -> 0.01 us
    pallas_call x0 -> x4, Pallas kernels: none -> 9.03 us  [the longest x1 5.31 us: body(): pl.pallas_call(product_kernel, grid=(DBLK // STEP_ROWS,), in_specs=[pl.Bl...]
    scatter x1 -> x0, local copies, waits for them, and re-layouts: 4.32 us -> none  [slot_buffers(): source = jnp.zeros((expert_count * capacity,), jnp.int32).at[target].set(...]
    select_n x3 -> x0, other arithmetic: 3.34 us -> none  [the longest x1 2.18 us: slot_buffers(): jnp.where(filled[:, None], rows_x[slot_index // top_count], jnp.zeros((),...]
  transfers between devices with their start and end apart: 3 -> 3, of which waited for: 3 -> 2; matrix products, arithmetic and copies ran while one was open for 17% -> 2% of each run, Pallas kernels for 0% -> 3%
where the time goes in v1:
time: 114 us
  waiting for transfers between devices  35.9 us (31%)
  starting transfers between devices  27.6 us (24%)
  blocking collectives  19.3 us (17%)
  between operations  13.5 us (12%)
  Pallas kernels  9.03 us (8%)
  local copies, waits for them, and re-layouts  7.2 us (6%)
    all_to_all x1, starting transfers between devices, body(): lax.all_to_all(send, ('y', 'z'), split_axis=0, concat_axis=0, tiled=True)  24 us
    all_to_all x1, waiting for transfers between devices, body(): lax.all_to_all(jnp.broadcast_to(routed[None], (DB, OWNERS, HALF, LANES)),...  23.6 us
    all_to_all x1, blocking collectives, body(): lax.all_to_all(routed.reshape(OWNERS, HALF, LANES), ('x', 'core'), split_...  19.3 us
    all_to_all x1, waiting for transfers between devices, body(): lax.all_to_all(send, ('y', 'z'), split_axis=0, concat_axis=0, tiled=True)  12.3 us
    pallas_call x1, Pallas kernels, body(): pl.pallas_call(product_kernel, grid=(DBLK // STEP_ROWS,), in_specs=[pl.Bl...  5.31 us
    unnamed x6, local copies, waits for them, and re-layouts  3.6 us
    all_to_all x1, starting transfers between devices, body(): lax.all_to_all(jnp.broadcast_to(routed[None], (DB, OWNERS, HALF, LANES)),...  3.57 us
  transfers between devices with their start and end apart: 3, of which 2 were waited for; matrix products, arithmetic and copies ran while one was open for 2% of the time, Pallas kernels for 3%

profile of v1, /device:TPU:1, one launch (start us, length us, event | category | flops | bytes accessed | tf_op | source)
XLA Modules:
  0.0 113.6 jit_solution(15657097961929897471)
XLA Ops:
  6.5 0.0 copy-start.1
  6.5 1.1 reshape_squeeze.7
  7.6 0.2 copy.12
  7.8 0.2 concatenate.15
  8.0 0.8 copy.21
  8.8 0.1 broadcast_in_dim.6
  8.9 1.0 pad_maximum_fusion
  9.9 24.0 %all-to-all-start = ((bf16[64,2,1152]{2,1,0:T(2,128)(2,1)}), bf16[64,2,1152]{2,1,0:T(2,128)(2,1)S(1)}, u32[]{:S(2)}, u32[]{:S(2)}) async-start(bf16[64,2,1152]{2,1,0:T(2,128)(2,1)} %pad_maximum_fusion), calls=%async_computation | async-start | bytes 589824 | tf_op jit(solution)/shard_map/all_to_all | solution.py:120
  33.8 0.0 all-gather.3.cloned.1.call-start
  33.9 0.8 copy.13
  34.7 12.3 %all-to-all-done = bf16[64,2,1152]{2,1,0:T(2,128)(2,1)S(1)} async-done(((bf16[64,2,1152]{2,1,0:T(2,128)(2,1)}), bf16[64,2,1152]{2,1,0:T(2,128)(2,1)S(1)}, u32[]{:S(2)}, u32[]{:S(2)}) %all-to-all-start) | async-done | bytes 294944 | tf_op jit(solution)/shard_map/all_to_all | solution.py:120
  47.0 0.1 reshape.26
  47.2 0.8 copy.14
  48.0 0.0 all-gather.3.cloned.1.call-update
  48.0 0.0 copy-done.1
  48.1 1.7 %shard_map.37.onehot_ref = bf16[384,4096]{1,0:T(8,128)(2,1)S(1)} custom-call(s32[8,128]{1,0:T(8,128)S(1)} %bitcast.38), custom_call_target="tpu_custom_call" | custom-call | tf_op jit(solution)/shard_map/pallas_call | solution.py:109
  49.8 1.0 shard_map.38
  50.8 19.3 %all_to_all.15 = bf16[16,24,128]{2,1,0:T(8,128)(2,1)S(1)} all-to-all(bf16[16,24,128]{2,1,0:T(8,128)(2,1)S(1)} %bitcast.37), channel_id=1, replica_groups=mesh['y'=8,'z'=8,'x'=8,'core'=2] {'x','core'}, dimensions={0} | all-to-all | bytes 196608 | tf_op jit(solution)/shard_map/all_to_all | solution.py:132
  70.1 1.0 broadcast_in_dim.7
  71.1 3.6 %all-to-all-start.2 = ((bf16[8,16,24,128]{3,2,1,0:T(8,128)(2,1)}), bf16[8,16,24,128]{3,2,1,0:T(8,128)(2,1)S(1)}, u32[]{:S(2)}, u32[]{:S(2)}) async-start(bf16[8,16,24,128]{3,2,1,0:T(8,128)(2,1)} %broadcast_in_dim.7), calls=%async_computation.2 | async-start | bytes 1572864 | tf_op jit(solution)/shard_map/all_to_all | solution.py:135
  74.7 23.6 %all-to-all-done.2 = bf16[8,16,24,128]{3,2,1,0:T(8,128)(2,1)S(1)} async-done(((bf16[8,16,24,128]{3,2,1,0:T(8,128)(2,1)}), bf16[8,16,24,128]{3,2,1,0:T(8,128)(2,1)S(1)}, u32[]{:S(2)}, u32[]{:S(2)}) %all-to-all-start.2) | async-done | bytes 786464 | tf_op jit(solution)/shard_map/all_to_all | solution.py:135
  98.3 1.0 shard_map.39
  99.3 0.1 copy.16
  99.3 0.0 all-gather.3.cloned.1.call-done
  99.4 0.0 copy-start
  99.4 2.0 %copy-done = bf16[14592,128]{1,0:T(8,128)(2,1)S(1)} copy-done((bf16[14592,128]{1,0:T(8,128)(2,1)S(1)}, bf16[14592,128]{1,0:T(8,128)(2,1)}, u32[]{:S(2)}) %copy-start) | copy-done | bytes 3735576
  101.4 5.3 %shard_map.40 = bf16[2,896,256]{2,1,0:T(8,128)(2,1)} custom-call(s32[1]{0:T(128)} %bitcast.first_ref, bf16[16,912,128]{2,1,0:T(8,128)(2,1)S(1)} %bitcast.32, bf16[16,912,128]{2,1,0:T(8,128)(2,1)S(1)} %bitcast.33, bf16[2,16,48,256]{3,2,1,0:T(8,128)(2,1)S(1)} %bitcast.34), custom_call_target="tpu_custom_call" | custom-call | tf_op jit(solution)/shard_map/pallas_call | solution.py:151
  (5 shorter events, 0.1 us)
Async XLA Ops:
  6.5 41.5 %copy-start.1 = (s32[1,128,8]{1,2,0:T(8,128)S(1)}, s32[1,128,8]{1,2,0:T(8,128)}, u32[]{:S(2)}) copy-start(s32[1,128,8]{1,2,0:T(8,128)} %param.5) | copy-start | bytes 12292
  9.9 37.1 %all-to-all-start = ((bf16[64,2,1152]{2,1,0:T(2,128)(2,1)}), bf16[64,2,1152]{2,1,0:T(2,128)(2,1)S(1)}, u32[]{:S(2)}, u32[]{:S(2)}) async-start(bf16[64,2,1152]{2,1,0:T(2,128)(2,1)} %pad_maximum_fusion), calls=%async_computation | async-start | bytes 589824 | tf_op jit(solution)/shard_map/all_to_all | solution.py:120
  33.8 65.5 %all-gather.3.cloned.1.call-start = ((), (), s32[]{:S(2)}) async-start(), calls=%async_computation.3 | async-start | bytes 3969024 | tf_op jit(solution)/shard_map/all_gather | solution.py:125
  71.1 27.2 %all-to-all-start.2 = ((bf16[8,16,24,128]{3,2,1,0:T(8,128)(2,1)}), bf16[8,16,24,128]{3,2,1,0:T(8,128)(2,1)S(1)}, u32[]{:S(2)}, u32[]{:S(2)}) async-start(bf16[8,16,24,128]{3,2,1,0:T(8,128)(2,1)} %broadcast_in_dim.7), calls=%async_computation.2 | async-start | bytes 1572864 | tf_op jit(solution)/shard_map/all_to_all | solution.py:135
  99.4 2.1 %copy-start = (bf16[14592,128]{1,0:T(8,128)(2,1)S(1)}, bf16[14592,128]{1,0:T(8,128)(2,1)}, u32[]{:S(2)}) copy-start(bf16[14592,128]{1,0:T(8,128)(2,1)} %all-gather.3.cloned.1.call-done) | copy-start | bytes 11206660
Sparse Core Ops, SparseCore 0:
  48.2 42.9 all-gather.2

commit v2 on v1

v2 whole, which is shorter than its diff:
```python
import jax
import jax.numpy as jnp
from jax import lax
from jax.experimental import pallas as pl
from jax.experimental.pallas import tpu as pltpu
from jax.sharding import Mesh, PartitionSpec as P

DB = 8
FB = 8
TOP = 8
TOK = 128
DBLK = 896
FBLK = 256
PIECE = FBLK // DB
EXPERTS = 32
CAP = 48
OWN = 2
OWNERS = 16
HALF = CAP // 2
LANES = 128
SWAP = DBLK // 2
PART = 128


def earlier():
    row = lax.broadcasted_iota(jnp.int32, (TOK, TOK), 0)
    col = lax.broadcasted_iota(jnp.int32, (TOK, TOK), 1)
    return (row < col).astype(jnp.bfloat16)


def place_kernel(ids_ref, onehot_ref):
    expert = lax.broadcasted_iota(jnp.int32, (EXPERTS, TOK), 0)
    named = jnp.zeros((EXPERTS, TOK), jnp.float32)
    for k in range(TOP):
        named += (ids_ref[k : k + 1, :] == expert).astype(jnp.float32)
    before = jnp.dot(named.astype(jnp.bfloat16), earlier(), preferred_element_type=jnp.float32)
    place = before.astype(jnp.int32) + CAP * expert
    row = lax.broadcasted_iota(jnp.int32, (OWNERS * HALF, TOK), 0)
    owner = row // HALF
    base = owner * (OWN * CAP) + (row - owner * HALF)
    for k in range(TOP):
        target = jnp.sum(
            jnp.where(ids_ref[k : k + 1, :] == expert, place, 0), axis=0, keepdims=True
        )
        for j in range(4):
            at = (j * TOP + k) * TOK
            onehot_ref[:, at : at + TOK] = (base + j * HALF == target).astype(jnp.bfloat16)


def pack_kernel(got_ref, onehot_ref, ids_ref, first_ref, left_ref):
    left = got_ref[:, :DBLK].T
    left_ref[...] = left
    pieces = got_ref[:, DBLK:].astype(jnp.float32)
    block = lax.broadcasted_iota(jnp.int32, (TOK, LANES), 1) // PIECE
    rows = []
    for j in range(4):
        for k in range(TOP):
            half = pieces[:, (k // 4) * LANES : (k // 4 + 1) * LANES]
            shift = ((j - k) % 4) * PIECE
            moved = pltpu.roll(half, shift, 1) if shift else half
            rows.append(jnp.where(block == j, moved, 0.0).astype(jnp.bfloat16))
    routed = jnp.dot(
        onehot_ref[...], jnp.concatenate(rows, axis=0), preferred_element_type=jnp.float32
    )
    ids = ids_ref[...].astype(jnp.float32)
    for d in range(OWNERS):
        at = (d % 2) * SWAP
        first_ref[d, :PART, :] = left[at : at + PART]
        first_ref[d, PART:, :] = jnp.concatenate(
            [routed[d * HALF : (d + 1) * HALF], ids], axis=0
        ).astype(jnp.bfloat16)


def dense_kernel(info_ref, ids_ref, *refs):
    dense_ref = refs[DB]
    slots = jnp.concatenate([refs[s][...] for s in range(DB)], axis=1)
    source = lax.broadcasted_iota(jnp.int32, (DB * LANES, FBLK), 0)
    column = lax.broadcasted_iota(jnp.int32, (DB * LANES, FBLK), 1)
    lane = source % LANES
    wanted = ((info_ref[1] + DB - source // LANES) % DB) * PIECE + lane % PIECE
    spread = []
    for j in range(4):
        pick = ((column == wanted) & (lane // PIECE == j)).astype(jnp.bfloat16)
        spread.append(jnp.dot(slots, pick, preferred_element_type=jnp.float32))
    named = []
    for e in range(OWN):
        for g in range(OWNERS):
            hit = (ids_ref[g].astype(jnp.int32) == info_ref[0] + e).astype(jnp.float32)
            named.append(jnp.sum(hit, axis=0, keepdims=True))
    named = jnp.concatenate(named, axis=0)
    before = jnp.dot(named.astype(jnp.bfloat16), earlier(), preferred_element_type=jnp.float32)
    place = jnp.where(named > 0.0, before, -1.0).T
    number = lax.broadcasted_iota(jnp.int32, (TOK, CAP), 1).astype(jnp.float32)
    for e in range(OWN):
        for g in range(OWNERS):
            at = e * OWNERS + g
            pick = (place[:, at : at + 1] == number).astype(jnp.bfloat16)
            rows = slice(g * HALF, (g + 1) * HALF)
            value = jnp.concatenate([spread[2 * e][rows], spread[2 * e + 1][rows]], axis=0)
            dense_ref[g * TOK : (g + 1) * TOK, e * FBLK : (e + 1) * FBLK] = jnp.dot(
                pick, value.astype(jnp.bfloat16), preferred_element_type=jnp.float32
            ).astype(jnp.bfloat16)


def product_kernel(side_ref, first_ref, rest_ref, dense_ref, *refs):
    del side_ref
    out_ref = refs[-1]
    left = [jnp.concatenate([first_ref[g], rest_ref[g]], axis=0) for g in range(OWNERS)]
    total = jnp.dot(
        jnp.concatenate(left, axis=1), dense_ref[...], preferred_element_type=jnp.float32
    )
    for e in range(OWN):
        out_ref[e] = total[:, e * FBLK : (e + 1) * FBLK].astype(jnp.bfloat16)


def params(mib):
    return pltpu.CompilerParams(vmem_limit_bytes=mib << 20)


def cost(flops, size):
    return pl.CostEstimate(flops=flops, bytes_accessed=size, transcendentals=0)


def product(side, first, rest, dense, out):
    specs = [
        pl.BlockSpec((OWNERS, PART, TOK), lambda i, s: (0, 0, 0)),
        pl.BlockSpec((OWNERS, SWAP - PART, TOK), lambda i, s: (0, 0, 0)),
        pl.BlockSpec((OWNERS * TOK, OWN * FBLK), lambda i, s: (0, 0)),
    ]
    args = [side, first, rest, dense]
    if out is not None:
        specs.append(pl.BlockSpec(memory_space=pl.ANY))
        args.append(out)
    return pl.pallas_call(
        product_kernel,
        grid_spec=pltpu.PrefetchScalarGridSpec(
            num_scalar_prefetch=1,
            grid=(1,),
            in_specs=specs,
            out_specs=pl.BlockSpec((OWN, SWAP, FBLK), lambda i, s: (0, s[0], 0)),
        ),
        out_shape=jax.ShapeDtypeStruct((OWN, DBLK, FBLK), jnp.bfloat16),
        input_output_aliases={} if out is None else {4: 0},
        cost_estimate=cost(2 * SWAP * 2048 * 512, 5 << 20),
        compiler_params=params(32),
    )(*args)


def body(tokens, slot_grads, expert_ids):
    ids = expert_ids[0].T
    onehot = pl.pallas_call(
        place_kernel,
        out_shape=jax.ShapeDtypeStruct((OWNERS * HALF, 4 * TOP * TOK), jnp.bfloat16),
        cost_estimate=cost(1 << 22, 6 << 20),
        compiler_params=params(16),
    )(ids)

    x_part = tokens[0].reshape(2, DB, DBLK).transpose(1, 0, 2)
    x_part = jnp.broadcast_to(x_part[:, None], (DB, FB, 2, DBLK))
    g_part = slot_grads[0].reshape(2, TOP, FB, DB, PIECE).transpose(3, 2, 0, 1, 4)
    g_part = g_part.reshape(DB, FB, 2, TOP * PIECE)
    send = jnp.concatenate([x_part, g_part], axis=3).reshape(DB * FB, 2, DBLK + FBLK)
    got = lax.all_to_all(send, ("y", "z"), split_axis=0, concat_axis=0, tiled=True)
    got = got.reshape(TOK, DBLK + FBLK)

    first, left = pl.pallas_call(
        pack_kernel,
        out_shape=(
            jax.ShapeDtypeStruct((OWNERS, PART + 32, TOK), jnp.bfloat16),
            jax.ShapeDtypeStruct((DBLK, TOK), jnp.bfloat16),
        ),
        cost_estimate=cost(1 << 29, 6 << 20),
        compiler_params=params(32),
    )(got, onehot, ids)
    owner = ("x", "core")
    first = lax.all_to_all(first, owner, split_axis=0, concat_axis=0, tiled=True)
    rest = left.reshape(2, SWAP, TOK)[:, PART:]
    rest = jnp.broadcast_to(rest[None], (8, 2, SWAP - PART, TOK)).reshape(OWNERS, SWAP - PART, TOK)
    group_ids = first[:, PART + HALF :]
    rest, group_ids = lax.optimization_barrier((rest, group_ids))
    rest = lax.all_to_all(rest, owner, split_axis=0, concat_axis=0, tiled=True)

    routed = first[:, PART : PART + HALF].reshape(OWNERS * HALF, LANES)
    slots = [routed] + [
        lax.ppermute(routed, "y", [(i, (i + s) % DB) for i in range(DB)]) for s in range(1, DB)
    ]
    across = [(0, 1), (1, 0)]
    own = first[:, :PART]
    first_across = lax.ppermute(own, "core", across)
    core = lax.axis_index("core")
    info = jnp.stack([OWN * lax.axis_index(owner), lax.axis_index("y")]).astype(jnp.int32)
    dense = pl.pallas_call(
        dense_kernel,
        in_specs=[pl.BlockSpec(memory_space=pltpu.SMEM)]
        + [pl.BlockSpec(memory_space=pltpu.VMEM)] * (DB + 1),
        out_shape=jax.ShapeDtypeStruct((OWNERS * TOK, OWN * FBLK), jnp.bfloat16),
        cost_estimate=cost(1 << 30, 4 << 20),
        compiler_params=params(32),
    )(info, group_ids, *slots)

    rest, dense = lax.optimization_barrier((rest, dense))
    rest_across = lax.ppermute(rest, "core", across)
    side = core.astype(jnp.int32).reshape(1)
    out = product(side, own, rest, dense, None)
    out = product(1 - side, first_across, rest_across, dense, out)
    return out[:, None]


def solution(mesh):
    grid = Mesh(mesh.devices.reshape(DB, FB, 8, 2), ("y", "z", "x", "core"))
    owner, block = ("x", "core"), ("y", "z")
    placed = (P(owner, block, None), P(owner, block, None, None), P(owner, None, None))
    return jax.shard_map(
        body, mesh=grid, in_specs=placed, out_specs=P(owner, block, None, None), check_vma=False
    )
```

time: 114 us -> 128 us (1.12)
  starting transfers between devices: 27.6 us -> 66.4 us
  blocking collectives: 19.3 us -> 0 us
  between operations: 13.5 us -> 0.27 us
  waiting for transfers between devices: 35.9 us -> 40.5 us
  local copies, waits for them, and re-layouts: 7.2 us -> 10.4 us
    ppermute x0 -> x9, starting transfers between devices: none -> 28.5 us  [the longest x7 24.2 us: body(): lax.ppermute(routed, 'y', [(i, (i + s) % DB) for i in range(DB)])]
    all_to_all x1 -> x0, blocking collectives: 19.3 us -> none  [body(): lax.all_to_all(routed.reshape(OWNERS, HALF, LANES), ('x', 'core'), split_...]
    all_to_all x1 -> x2, starting transfers between devices: 3.57 us -> 13.6 us  [the longest x1 10 us: body(): lax.all_to_all(first, owner, split_axis=0, concat_axis=0, tiled=True)]
    ppermute x0 -> x9, waiting for transfers between devices: none -> 9.16 us  [the longest x7 9.15 us: body(): lax.ppermute(routed, 'y', [(i, (i + s) % DB) for i in range(DB)])]
    all_to_all x1 -> x2, waiting for transfers between devices: 23.6 us -> 20 us  [the longest x1 20 us: body(): lax.all_to_all(first, owner, split_axis=0, concat_axis=0, tiled=True)]
    unnamed x6 -> x19, local copies, waits for them, and re-layouts: 3.6 us -> 5.33 us
    pallas_call x3 -> x4, Pallas kernels: 7.33 us -> 7.34 us  [the longest x2 3.76 us: product(): pl.pallas_call(product_kernel, grid_spec=pltpu.PrefetchScalarGridSpec(num...]
  transfers between devices with their start and end apart: 3 -> 12, of which waited for: 2 -> 4; matrix products, arithmetic and copies ran while one was open for 2% -> 1% of each run, Pallas kernels for 3% -> 5%
where the time goes in v2:
time: 128 us
  starting transfers between devices  66.4 us (52%)
  waiting for transfers between devices  40.5 us (32%)
  local copies, waits for them, and re-layouts  10.4 us (8%)
  Pallas kernels  9.04 us (7%)
    ppermute x7, starting transfers between devices, body(): lax.ppermute(routed, 'y', [(i, (i + s) % DB) for i in range(DB)])  24.2 us
    all_to_all x1, starting transfers between devices, body(): lax.all_to_all(send, ('y', 'z'), split_axis=0, concat_axis=0, tiled=True)  24.2 us
    all_to_all x1, waiting for transfers between devices, body(): lax.all_to_all(first, owner, split_axis=0, concat_axis=0, tiled=True)  20 us
    all_to_all x1, waiting for transfers between devices, body(): lax.all_to_all(send, ('y', 'z'), split_axis=0, concat_axis=0, tiled=True)  11.3 us
    all_to_all x1, starting transfers between devices, body(): lax.all_to_all(first, owner, split_axis=0, concat_axis=0, tiled=True)  10 us
    ppermute x7, waiting for transfers between devices, body(): lax.ppermute(routed, 'y', [(i, (i + s) % DB) for i in range(DB)])  9.15 us
    unnamed x19, local copies, waits for them, and re-layouts  5.33 us
    pallas_call x2, Pallas kernels, product(): pl.pallas_call(product_kernel, grid_spec=pltpu.PrefetchScalarGridSpec(num...  3.76 us
  transfers between devices with their start and end apart: 12, of which 4 were waited for; matrix products, arithmetic and copies ran while one was open for 1% of the time, Pallas kernels for 5%

profile of v2, /device:TPU:1, one launch (start us, length us, event | category | flops | bytes accessed | tf_op | source)
XLA Modules:
  0.0 127.6 jit_solution(16558520918545692132)
XLA Ops:
  0.0 0.8 copy.10
  0.8 1.1 reshape_squeeze.7
  2.4 1.0 pad_maximum_fusion
  3.3 24.2 %all-to-all-start = ((bf16[64,2,1152]{2,1,0:T(2,128)(2,1)}), bf16[64,2,1152]{2,1,0:T(2,128)(2,1)}, u32[]{:S(2)}, u32[]{:S(2)}) async-start(bf16[64,2,1152]{2,1,0:T(2,128)(2,1)} %pad_maximum_fusion), calls=%async_computation | async-start | bytes 589824 | tf_op jit(solution)/shard_map/all_to_all | solution.py:163
  27.6 1.7 %shard_map.37.onehot_ref = bf16[384,4096]{1,0:T(8,128)(2,1)S(1)} custom-call(s32[8,128]{1,0:T(8,128)S(1)} %bitcast.35), custom_call_target="tpu_custom_call" | custom-call | flops 4194304 | bytes 6291456 | tf_op jit(solution)/shard_map/pallas_call | solution.py:151
  29.3 11.3 %all-to-all-done = bf16[64,2,1152]{2,1,0:T(2,128)(2,1)} async-done(((bf16[64,2,1152]{2,1,0:T(2,128)(2,1)}), bf16[64,2,1152]{2,1,0:T(2,128)(2,1)}, u32[]{:S(2)}, u32[]{:S(2)}) %all-to-all-start) | async-done | bytes 294944 | tf_op jit(solution)/shard_map/all_to_all | solution.py:163
  40.6 1.1 reshape.23.got_ref
  41.6 1.0 shard_map.38
  42.7 0.8 copy-done
  43.5 0.7 copy-done.1
  44.2 10.0 %all-to-all-start.1 = ((bf16[16,160,128]{2,1,0:T(8,128)(2,1)}), bf16[16,160,128]{2,1,0:T(8,128)(2,1)S(1)}, u32[]{:S(2)}, u32[]{:S(2)}) async-start(bf16[16,160,128]{2,1,0:T(8,128)(2,1)} %copy-done), calls=%async_computation.1 | async-start | bytes 1310720 | tf_op jit(solution)/shard_map/all_to_all | solution.py:176
  54.3 20.0 %all-to-all-done.1 = bf16[16,160,128]{2,1,0:T(8,128)(2,1)S(1)} async-done(((bf16[16,160,128]{2,1,0:T(8,128)(2,1)}), bf16[16,160,128]{2,1,0:T(8,128)(2,1)S(1)}, u32[]{:S(2)}, u32[]{:S(2)}) %all-to-all-start.1) | async-done | bytes 655392 | tf_op jit(solution)/shard_map/all_to_all | solution.py:176
  74.3 1.3 %broadcast_in_dim.7 = bf16[8,2,320,128]{3,2,1,0:T(8,128)(2,1)} broadcast(bf16[2,320,128]{2,1,0:T(8,128)(2,1)S(1)} %slice.17), dimensions={1,2,3} | broadcast | bytes 1474560 | tf_op jit(solution)/shard_map/broadcast_in_dim | solution.py:178
  75.6 3.6 %all-to-all-start.2 = ((bf16[16,320,128]{2,1,0:T(8,128)(2,1)}), bf16[16,320,128]{2,1,0:T(8,128)(2,1)S(1)}, u32[]{:S(2)}, u32[]{:S(2)}) async-start(bf16[16,320,128]{2,1,0:T(8,128)(2,1)} %bitcast.7), calls=%async_computation.2 | async-start | bytes 2621440 | tf_op jit(solution)/shard_map/all_to_all | solution.py:181
  79.3 2.5 %collective-permute-start.7 = (bf16[384,128]{1,0:T(8,128)(2,1)S(1)}, bf16[384,128]{1,0:T(8,128)(2,1)S(1)}, u32[]{:S(2)}, u32[]{:S(2)}) collective-permute-start(bf16[384,128]{1,0:T(8,128)(2,1)S(1)} %bitcast.27), channel_id=1, source_target_pairs={{0,896},{128,0},{256,128},{384,256},{512,384},{640,512},{768,640},... | collective-permute-start | bytes 294920 | tf_op jit(solution)/shard_map/ppermute | solution.py:185
  81.7 2.5 %collective-permute-start.6 = (bf16[384,128]{1,0:T(8,128)(2,1)S(1)}, bf16[384,128]{1,0:T(8,128)(2,1)S(1)}, u32[]{:S(2)}, u32[]{:S(2)}) collective-permute-start(bf16[384,128]{1,0:T(8,128)(2,1)S(1)} %bitcast.28), channel_id=1, source_target_pairs={{0,768},{128,896},{256,0},{384,128},{512,256},{640,384},{768,512},... | collective-permute-start | bytes 294920 | tf_op jit(solution)/shard_map/ppermute | solution.py:185
  84.2 5.9 %collective-permute-start.5 = (bf16[384,128]{1,0:T(8,128)(2,1)S(1)}, bf16[384,128]{1,0:T(8,128)(2,1)S(1)}, u32[]{:S(2)}, u32[]{:S(2)}) collective-permute-start(bf16[384,128]{1,0:T(8,128)(2,1)S(1)} %bitcast.29), channel_id=1, source_target_pairs={{0,640},{128,768},{256,896},{384,0},{512,128},{640,256},{768,384},... | collective-permute-start | bytes 294920 | tf_op jit(solution)/shard_map/ppermute | solution.py:185
  90.1 3.5 %collective-permute-start.4 = (bf16[384,128]{1,0:T(8,128)(2,1)S(1)}, bf16[384,128]{1,0:T(8,128)(2,1)S(1)}, u32[]{:S(2)}, u32[]{:S(2)}) collective-permute-start(bf16[384,128]{1,0:T(8,128)(2,1)S(1)} %bitcast.30), channel_id=1, source_target_pairs={{0,512},{128,640},{256,768},{384,896},{512,0},{640,128},{768,256},... | collective-permute-start | bytes 294920 | tf_op jit(solution)/shard_map/ppermute | solution.py:185
  93.6 3.3 %collective-permute-start.3 = (bf16[384,128]{1,0:T(8,128)(2,1)S(1)}, bf16[384,128]{1,0:T(8,128)(2,1)S(1)}, u32[]{:S(2)}, u32[]{:S(2)}) collective-permute-start(bf16[384,128]{1,0:T(8,128)(2,1)S(1)} %bitcast.31), channel_id=1, source_target_pairs={{0,384},{128,512},{256,640},{384,768},{512,896},{640,0},{768,128},... | collective-permute-start | bytes 294920 | tf_op jit(solution)/shard_map/ppermute | solution.py:185
  97.5 4.7 %collective-permute-start.2 = (bf16[384,128]{1,0:T(8,128)(2,1)S(1)}, bf16[384,128]{1,0:T(8,128)(2,1)S(1)}, u32[]{:S(2)}, u32[]{:S(2)}) collective-permute-start(bf16[384,128]{1,0:T(8,128)(2,1)S(1)} %bitcast.32), channel_id=1, source_target_pairs={{0,256},{128,384},{256,512},{384,640},{512,768},{640,896},{768,0},... | collective-permute-start | bytes 294920 | tf_op jit(solution)/shard_map/ppermute | solution.py:185
  102.3 0.6 copy-done.6
  102.9 1.9 %collective-permute-start.1 = (bf16[384,128]{1,0:T(8,128)(2,1)S(1)}, bf16[384,128]{1,0:T(8,128)(2,1)S(1)}, u32[]{:S(2)}, u32[]{:S(2)}) collective-permute-start(bf16[384,128]{1,0:T(8,128)(2,1)S(1)} %bitcast.33), channel_id=1, source_target_pairs={{0,128},{128,256},{256,384},{384,512},{512,640},{640,768},{768,896... | collective-permute-start | bytes 294920 | tf_op jit(solution)/shard_map/ppermute | solution.py:185
  104.9 5.0 %collective-permute-done.3.refs_3_ = bf16[384,128]{1,0:T(8,128)(2,1)S(1)} collective-permute-done((bf16[384,128]{1,0:T(8,128)(2,1)S(1)}, bf16[384,128]{1,0:T(8,128)(2,1)S(1)}, u32[]{:S(2)}, u32[]{:S(2)}) %collective-permute-start.3) | collective-permute-done | bytes 98336 | tf_op jit(solution)/shard_map/ppermute | solution.py:185
  109.9 4.2 %collective-permute-done.1.refs_1_ = bf16[384,128]{1,0:T(8,128)(2,1)S(1)} collective-permute-done((bf16[384,128]{1,0:T(8,128)(2,1)S(1)}, bf16[384,128]{1,0:T(8,128)(2,1)S(1)}, u32[]{:S(2)}, u32[]{:S(2)}) %collective-permute-start.1) | collective-permute-done | bytes 98336 | tf_op jit(solution)/shard_map/ppermute | solution.py:185
  114.1 0.9 copy-done.5
  115.0 0.9 copy-done.7
  115.9 2.5 %shard_map.39.dense_ref = bf16[2048,512]{1,0:T(8,128)(2,1)S(1)} custom-call(s32[2]{0:T(128)S(1)} %pad_add_fusion.info_ref, bf16[16,8,128]{2,1,0:T(8,128)(2,1)S(1)} %slice.18.ids_ref, bf16[384,128]{1,0:T(8,128)(2,1)S(1)} %bitcast.34, bf16[384,128]{1,0:T(8,128)(2,1)S(1)} %collective-permute-done.1.refs_1_, ...), custom_call_target="tpu_custom_call" | custom-call | flops 1073741824 | bytes 4194304 | tf_op jit(solution)/shard_map/pallas_call | solution.py:192
  118.4 2.4 %collective-permute-start.8 = (bf16[16,320,128]{2,1,0:T(8,128)(2,1)S(1)}, bf16[16,320,128]{2,1,0:T(8,128)(2,1)S(1)}, u32[]{:S(2)}, u32[]{:S(2)}) collective-permute-start(bf16[16,320,128]{2,1,0:T(8,128)(2,1)S(1)} %all-to-all-done.2.rest_ref), channel_id=1, source_target_pairs={{0,1},{1,0},{2,3},{3,2},{4,5},{5,4},{6,7},{7,6},{8,9},{9,8},{10,11... | collective-permute-start | bytes 3932168 | tf_op jit(solution)/shard_map/ppermute | solution.py:202
  120.8 1.1 slice.16.first_ref
  121.9 1.9 %collective-permute-start = (bf16[16,128,128]{2,1,0:T(8,128)(2,1)S(1)}, bf16[16,128,128]{2,1,0:T(8,128)(2,1)S(1)}, u32[]{:S(2)}, u32[]{:S(2)}) collective-permute-start(bf16[16,128,128]{2,1,0:T(8,128)(2,1)S(1)} %slice.16.first_ref), channel_id=1, source_target_pairs={{0,1},{1,0},{2,3},{3,2},{4,5},{5,4},{6,7},{7,6},{8,9},{9,8},{10,11... | collective-permute-start | bytes 1572872 | tf_op jit(solution)/shard_map/ppermute | solution.py:189
  123.8 1.9 %shard_map.40.refs_0_ = bf16[2,896,256]{2,1,0:T(8,128)(2,1)} custom-call(s32[1]{0:T(128)} %bitcast.side_ref, bf16[16,128,128]{2,1,0:T(8,128)(2,1)S(1)} %slice.16.first_ref, bf16[16,320,128]{2,1,0:T(8,128)(2,1)S(1)} %all-to-all-done.2.rest_ref, bf16[2048,512]{1,0:T(8,128)(2,1)S(1)} %shard_map.39.dense_ref), custom_call_target="tpu_custom_call" | custom-call | flops 939524096 | bytes 5242880 | tf_op jit(solution)/shard_map/pallas_call | solution.py:134
  125.7 1.9 %shard_map.41 = bf16[2,896,256]{2,1,0:T(8,128)(2,1)} custom-call(s32[1]{0:T(128)S(6)} %sub.3.side_ref, bf16[16,128,128]{2,1,0:T(8,128)(2,1)S(1)} %collective-permute-done.first_ref, bf16[16,320,128]{2,1,0:T(8,128)(2,1)S(1)} %collective-permute-done.8.rest_ref, bf16[2048,512]{1,0:T(8,128)(2,1)S(1)} %shard_map.39.dense_ref, ...), custom_call_target="tpu_custom_call", output_to_operand_aliasing={{}: (4, {})} | custom-call | flops 939524096 | bytes 5242880 | tf_op jit(solution)/shard_map/pallas_call | solution.py:134
  (29 shorter events, 1.3 us)
Async XLA Ops:
  0.8 26.8 %copy-start.3 = (s32[1,128,8]{1,2,0:T(8,128)S(1)}, s32[1,128,8]{1,2,0:T(8,128)}, u32[]{:S(2)}) copy-start(s32[1,128,8]{1,2,0:T(8,128)} %param.5) | copy-start | bytes 12292
  3.3 37.2 %all-to-all-start = ((bf16[64,2,1152]{2,1,0:T(2,128)(2,1)}), bf16[64,2,1152]{2,1,0:T(2,128)(2,1)}, u32[]{:S(2)}, u32[]{:S(2)}) async-start(bf16[64,2,1152]{2,1,0:T(2,128)(2,1)} %pad_maximum_fusion), calls=%async_computation | async-start | bytes 589824 | tf_op jit(solution)/shard_map/all_to_all | solution.py:163
  42.7 0.8 copy-start
  43.5 0.7 copy-start.1
  44.2 10.0 %copy-start.2 = (bf16[896,128]{1,0:T(8,128)(2,1)S(1)}, bf16[896,128]{1,0:T(8,128)(2,1)}, u32[]{:S(2)}) copy-start(bf16[896,128]{1,0:T(8,128)(2,1)} %copy-done.1) | copy-start | bytes 688132
  44.2 30.1 %all-to-all-start.1 = ((bf16[16,160,128]{2,1,0:T(8,128)(2,1)}), bf16[16,160,128]{2,1,0:T(8,128)(2,1)S(1)}, u32[]{:S(2)}, u32[]{:S(2)}) async-start(bf16[16,160,128]{2,1,0:T(8,128)(2,1)} %copy-done), calls=%async_computation.1 | async-start | bytes 1310720 | tf_op jit(solution)/shard_map/all_to_all | solution.py:176
  74.3 4.9 %copy-start.8 = (bf16[16,160,128]{2,1,0:T(8,128)(2,1)}, bf16[16,160,128]{2,1,0:T(8,128)(2,1)S(1)}, u32[]{:S(2)}) copy-start(bf16[16,160,128]{2,1,0:T(8,128)(2,1)S(1)} %all-to-all-done.1) | copy-start | bytes 1966084
  75.6 42.8 %all-to-all-start.2 = ((bf16[16,320,128]{2,1,0:T(8,128)(2,1)}), bf16[16,320,128]{2,1,0:T(8,128)(2,1)S(1)}, u32[]{:S(2)}, u32[]{:S(2)}) async-start(bf16[16,320,128]{2,1,0:T(8,128)(2,1)} %bitcast.7), calls=%async_computation.2 | async-start | bytes 2621440 | tf_op jit(solution)/shard_map/all_to_all | solution.py:181
  79.3 17.6 %collective-permute-start.7 = (bf16[384,128]{1,0:T(8,128)(2,1)S(1)}, bf16[384,128]{1,0:T(8,128)(2,1)S(1)}, u32[]{:S(2)}, u32[]{:S(2)}) collective-permute-start(bf16[384,128]{1,0:T(8,128)(2,1)S(1)} %bitcast.27), channel_id=1, source_target_pairs={{0,896},{128,0},{256,128},{384,256},{512,384},{640,512},{768,640},... | collective-permute-start | bytes 294920 | tf_op jit(solution)/shard_map/ppermute | solution.py:185
  81.7 20.5 %collective-permute-start.6 = (bf16[384,128]{1,0:T(8,128)(2,1)S(1)}, bf16[384,128]{1,0:T(8,128)(2,1)S(1)}, u32[]{:S(2)}, u32[]{:S(2)}) collective-permute-start(bf16[384,128]{1,0:T(8,128)(2,1)S(1)} %bitcast.28), channel_id=1, source_target_pairs={{0,768},{128,896},{256,0},{384,128},{512,256},{640,384},{768,512},... | collective-permute-start | bytes 294920 | tf_op jit(solution)/shard_map/ppermute | solution.py:185
  84.2 20.7 %collective-permute-start.5 = (bf16[384,128]{1,0:T(8,128)(2,1)S(1)}, bf16[384,128]{1,0:T(8,128)(2,1)S(1)}, u32[]{:S(2)}, u32[]{:S(2)}) collective-permute-start(bf16[384,128]{1,0:T(8,128)(2,1)S(1)} %bitcast.29), channel_id=1, source_target_pairs={{0,640},{128,768},{256,896},{384,0},{512,128},{640,256},{768,384},... | collective-permute-start | bytes 294920 | tf_op jit(solution)/shard_map/ppermute | solution.py:185
  90.1 14.8 %collective-permute-start.4 = (bf16[384,128]{1,0:T(8,128)(2,1)S(1)}, bf16[384,128]{1,0:T(8,128)(2,1)S(1)}, u32[]{:S(2)}, u32[]{:S(2)}) collective-permute-start(bf16[384,128]{1,0:T(8,128)(2,1)S(1)} %bitcast.30), channel_id=1, source_target_pairs={{0,512},{128,640},{256,768},{384,896},{512,0},{640,128},{768,256},... | collective-permute-start | bytes 294920 | tf_op jit(solution)/shard_map/ppermute | solution.py:185
  93.6 16.3 %collective-permute-start.3 = (bf16[384,128]{1,0:T(8,128)(2,1)S(1)}, bf16[384,128]{1,0:T(8,128)(2,1)S(1)}, u32[]{:S(2)}, u32[]{:S(2)}) collective-permute-start(bf16[384,128]{1,0:T(8,128)(2,1)S(1)} %bitcast.31), channel_id=1, source_target_pairs={{0,384},{128,512},{256,640},{384,768},{512,896},{640,0},{768,128},... | collective-permute-start | bytes 294920 | tf_op jit(solution)/shard_map/ppermute | solution.py:185
  96.9 0.6 copy-start.4
  97.5 12.4 %collective-permute-start.2 = (bf16[384,128]{1,0:T(8,128)(2,1)S(1)}, bf16[384,128]{1,0:T(8,128)(2,1)S(1)}, u32[]{:S(2)}, u32[]{:S(2)}) collective-permute-start(bf16[384,128]{1,0:T(8,128)(2,1)S(1)} %bitcast.32), channel_id=1, source_target_pairs={{0,256},{128,384},{256,512},{384,640},{512,768},{640,896},{768,0},... | collective-permute-start | bytes 294920 | tf_op jit(solution)/shard_map/ppermute | solution.py:185
  102.3 0.6 copy-start.6
  102.9 11.1 %collective-permute-start.1 = (bf16[384,128]{1,0:T(8,128)(2,1)S(1)}, bf16[384,128]{1,0:T(8,128)(2,1)S(1)}, u32[]{:S(2)}, u32[]{:S(2)}) collective-permute-start(bf16[384,128]{1,0:T(8,128)(2,1)S(1)} %bitcast.33), channel_id=1, source_target_pairs={{0,128},{128,256},{256,384},{384,512},{512,640},{640,768},{768,896... | collective-permute-start | bytes 294920 | tf_op jit(solution)/shard_map/ppermute | solution.py:185
  114.1 0.9 copy-start.5
  115.0 0.9 copy-start.7
  118.4 7.3 %collective-permute-start.8 = (bf16[16,320,128]{2,1,0:T(8,128)(2,1)S(1)}, bf16[16,320,128]{2,1,0:T(8,128)(2,1)S(1)}, u32[]{:S(2)}, u32[]{:S(2)}) collective-permute-start(bf16[16,320,128]{2,1,0:T(8,128)(2,1)S(1)} %all-to-all-done.2.rest_ref), channel_id=1, source_target_pairs={{0,1},{1,0},{2,3},{3,2},{4,5},{5,4},{6,7},{7,6},{8,9},{9,8},{10,11... | collective-permute-start | bytes 3932168 | tf_op jit(solution)/shard_map/ppermute | solution.py:202
  121.9 3.8 %collective-permute-start = (bf16[16,128,128]{2,1,0:T(8,128)(2,1)S(1)}, bf16[16,128,128]{2,1,0:T(8,128)(2,1)S(1)}, u32[]{:S(2)}, u32[]{:S(2)}) collective-permute-start(bf16[16,128,128]{2,1,0:T(8,128)(2,1)S(1)} %slice.16.first_ref), channel_id=1, source_target_pairs={{0,1},{1,0},{2,3},{3,2},{4,5},{5,4},{6,7},{7,6},{8,9},{9,8},{10,11... | collective-permute-start | bytes 1572872 | tf_op jit(solution)/shard_map/ppermute | solution.py:189

commit v3 on v2

v3 whole, which is shorter than its diff:
```python
import jax
import jax.numpy as jnp
from jax import lax
from jax.experimental import pallas as pl
from jax.experimental.pallas import tpu as pltpu
from jax.sharding import Mesh, PartitionSpec as P

DB = 8
FB = 8
TOP = 8
TOK = 128
DBLK = 896
FBLK = 256
PIECE = FBLK // DB
EXPERTS = 32
CAP = 48
OWN = 2
OWNERS = 16
HALF = CAP // 2
LANES = 128
XS = 8
OWNER = ("x", "core")


def earlier():
    row = lax.broadcasted_iota(jnp.int32, (TOK, TOK), 0)
    col = lax.broadcasted_iota(jnp.int32, (TOK, TOK), 1)
    return (row < col).astype(jnp.bfloat16)


def place_kernel(ids_ref, onehot_ref):
    expert = lax.broadcasted_iota(jnp.int32, (EXPERTS, TOK), 0)
    named = jnp.zeros((EXPERTS, TOK), jnp.float32)
    for k in range(TOP):
        named += (ids_ref[k : k + 1, :] == expert).astype(jnp.float32)
    before = jnp.dot(named.astype(jnp.bfloat16), earlier(), preferred_element_type=jnp.float32)
    place = before.astype(jnp.int32) + CAP * expert
    row = lax.broadcasted_iota(jnp.int32, (OWNERS * HALF, TOK), 0)
    owner = row // HALF
    base = owner * (OWN * CAP) + (row - owner * HALF)
    for k in range(TOP):
        target = jnp.sum(
            jnp.where(ids_ref[k : k + 1, :] == expert, place, 0), axis=0, keepdims=True
        )
        for j in range(4):
            at = (j * TOP + k) * TOK
            onehot_ref[:, at : at + TOK] = (base + j * HALF == target).astype(jnp.bfloat16)


def route_kernel(pieces_ref, onehot_ref, ids_ref, out_ref):
    pieces = pieces_ref[...].astype(jnp.float32)
    block = lax.broadcasted_iota(jnp.int32, (TOK, LANES), 1) // PIECE
    rows = []
    for j in range(4):
        for k in range(TOP):
            half = pieces[:, (k // 4) * LANES : (k // 4 + 1) * LANES]
            shift = ((j - k) % 4) * PIECE
            moved = pltpu.roll(half, shift, 1) if shift else half
            rows.append(jnp.where(block == j, moved, 0.0).astype(jnp.bfloat16))
    routed = jnp.dot(
        onehot_ref[...], jnp.concatenate(rows, axis=0), preferred_element_type=jnp.float32
    )
    ids = ids_ref[...].astype(jnp.float32)
    for d in range(OWNERS):
        out_ref[d] = jnp.concatenate(
            [routed[d * HALF : (d + 1) * HALF], ids], axis=0
        ).astype(jnp.bfloat16)


def copies_kernel(routed_ref, after_ref, slots_ref):
    del after_ref
    for g in range(OWNERS):
        slots = routed_ref[g].astype(jnp.float32)[:HALF].astype(jnp.bfloat16)
        for y in range(DB):
            slots_ref[y, g] = slots


def both_kernel(mine_ref, other_ref, after_ref, out_ref):
    del after_ref
    out_ref[0] = mine_ref[...]
    out_ref[1] = other_ref[...]


def group_order(me):
    x, core = me // 2, me % 2
    step = 1 - 2 * core
    order = []
    for away, first in (
        (0, core),
        (-1, core),
        (1, 1 - core),
        (-2, core),
        (2, 1 - core),
        (-3, core),
        (3, 1 - core),
        (4, core),
    ):
        chip = (x + away * step + XS) % XS
        order += [2 * chip + first, 2 * chip + 1 - first]
    return order


def dense_kernel(me_ref, routed_ref, slots_ref, dense_ref, value_ref):
    source = lax.broadcasted_iota(jnp.int32, (DB * LANES, FBLK), 0)
    column = lax.broadcasted_iota(jnp.int32, (DB * LANES, FBLK), 1)
    lane = source % LANES
    wanted = (source // LANES) * PIECE + lane % PIECE
    slots = jnp.concatenate([slots_ref[y] for y in range(DB)], axis=1)
    spread = []
    for j in range(4):
        pick = ((column == wanted) & (lane // PIECE == j)).astype(jnp.bfloat16)
        spread.append(jnp.dot(slots, pick, preferred_element_type=jnp.float32))
    for e in range(OWN):
        for g in range(OWNERS):
            rows = slice(g * HALF, (g + 1) * HALF)
            value_ref[e, g] = jnp.concatenate(
                [spread[2 * e][rows], spread[2 * e + 1][rows]], axis=0
            ).astype(jnp.bfloat16)
    order = group_order(me_ref[0])
    named = []
    for e in range(OWN):
        for i in range(OWNERS):
            ids = routed_ref[order[i]].astype(jnp.float32)[HALF:].astype(jnp.int32)
            hit = (ids == OWN * me_ref[0] + e).astype(jnp.float32)
            named.append(jnp.sum(hit, axis=0, keepdims=True))
    named = jnp.concatenate(named, axis=0)
    before = jnp.dot(named.astype(jnp.bfloat16), earlier(), preferred_element_type=jnp.float32)
    place = jnp.where(named > 0.0, before, -1.0).T
    number = lax.broadcasted_iota(jnp.int32, (TOK, CAP), 1).astype(jnp.float32)
    for e in range(OWN):
        for i in range(OWNERS):
            at = e * OWNERS + i
            pick = (place[:, at : at + 1] == number).astype(jnp.bfloat16)
            dense_ref[i * TOK : (i + 1) * TOK, e * FBLK : (e + 1) * FBLK] = jnp.dot(
                pick, value_ref[e, order[i]], preferred_element_type=jnp.float32
            ).astype(jnp.bfloat16)


def product_kernel(dense_ref, *refs):
    out_ref = refs[-1]
    left = []
    for ref in refs[:-1]:
        left += [ref[i] for i in range(ref.shape[0])]
    total = jnp.dot(
        jnp.concatenate(left, axis=1), dense_ref[...], preferred_element_type=jnp.float32
    )
    for e in range(OWN):
        out_ref[e] = total[:, e * FBLK : (e + 1) * FBLK].astype(jnp.bfloat16)


def params(mib):
    return pltpu.CompilerParams(vmem_limit_bytes=mib << 20)


def cost(flops, size):
    return pl.CostEstimate(flops=flops, bytes_accessed=size, transcendentals=0)


def ahead(value, steps):
    pairs = []
    for x in range(XS):
        pairs += [(2 * x, 2 * ((x + steps) % XS)), (2 * x + 1, 2 * ((x - steps) % XS) + 1)]
    return lax.ppermute(value, OWNER, pairs)


def swap(value):
    return lax.ppermute(value, "core", [(0, 1), (1, 0)])


def body(tokens, slot_grads, expert_ids):
    ids = expert_ids[0].T
    onehot = pl.pallas_call(
        place_kernel,
        out_shape=jax.ShapeDtypeStruct((OWNERS * HALF, 4 * TOP * TOK), jnp.bfloat16),
        cost_estimate=cost(1 << 22, 6 << 20),
        compiler_params=params(16),
    )(ids)

    x_part = tokens[0].reshape(2, DB, DBLK).transpose(1, 0, 2)
    x_part = jnp.broadcast_to(x_part[:, None], (DB, FB, 2, DBLK))
    g_part = slot_grads[0].reshape(2, TOP, FB, DB, PIECE).transpose(3, 2, 0, 1, 4)
    g_part = g_part.reshape(DB, FB, 2, TOP * PIECE)
    send = jnp.concatenate([x_part, g_part], axis=3).reshape(DB * FB, 2, DBLK + FBLK)
    got = lax.all_to_all(send, ("y", "z"), split_axis=0, concat_axis=0, tiled=True)
    got = got.reshape(TOK, DBLK + FBLK)

    pieces = got[:, DBLK:]
    mine = got[:, :DBLK].T
    mine, pieces = lax.optimization_barrier((mine, pieces))
    other = swap(mine)
    here = pl.pallas_call(
        both_kernel,
        in_specs=[
            pl.BlockSpec(memory_space=pltpu.VMEM),
            pl.BlockSpec(memory_space=pltpu.VMEM),
            pl.BlockSpec(memory_space=pl.ANY),
        ],
        out_shape=jax.ShapeDtypeStruct((2, DBLK, TOK), jnp.bfloat16),
        cost_estimate=cost(1 << 20, 1 << 20),
        compiler_params=params(8),
    )(mine, other, onehot)
    near = ahead(here, 1)
    next_ = ahead(here, 2)
    third = ahead(next_, 1)
    far = ahead(next_, 2)

    routed = pl.pallas_call(
        route_kernel,
        out_shape=jax.ShapeDtypeStruct((OWNERS, HALF + TOP, LANES), jnp.bfloat16),
        cost_estimate=cost(1 << 29, 4 << 20),
        compiler_params=params(16),
    )(pieces, onehot, ids)
    routed, here = lax.optimization_barrier((routed, here))
    routed = lax.all_to_all(routed, OWNER, split_axis=0, concat_axis=0, tiled=True)
    slots = pl.pallas_call(
        copies_kernel,
        in_specs=[
            pl.BlockSpec(memory_space=pltpu.VMEM),
            pl.BlockSpec(memory_space=pl.ANY),
        ],
        out_shape=jax.ShapeDtypeStruct((DB, OWNERS, HALF, LANES), jnp.bfloat16),
        cost_estimate=cost(1 << 20, 1 << 20),
        compiler_params=params(16),
    )(routed, next_)
    slots = lax.all_to_all(slots, "y", split_axis=0, concat_axis=0, tiled=True)

    me = lax.axis_index(OWNER).astype(jnp.int32).reshape(1)
    dense = pl.pallas_call(
        dense_kernel,
        in_specs=[
            pl.BlockSpec(memory_space=pltpu.SMEM),
            pl.BlockSpec(memory_space=pltpu.VMEM),
            pl.BlockSpec(memory_space=pltpu.VMEM),
        ],
        out_shape=jax.ShapeDtypeStruct((OWNERS * TOK, OWN * FBLK), jnp.bfloat16),
        scratch_shapes=[pltpu.VMEM((OWN, OWNERS, CAP, FBLK), jnp.bfloat16)],
        cost_estimate=cost(1 << 30, 4 << 20),
        compiler_params=params(16),
    )(me, routed, slots.reshape(DB, OWNERS * HALF, LANES))

    parts = [here, near, swap(near), next_, swap(next_), third, swap(third), far]
    out = pl.pallas_call(
        product_kernel,
        out_shape=jax.ShapeDtypeStruct((OWN, DBLK, FBLK), jnp.bfloat16),
        cost_estimate=cost(2 * DBLK * 2048 * 512, 7 << 20),
        compiler_params=params(24),
    )(dense, *parts)
    return out[:, None]


def solution(mesh):
    grid = Mesh(mesh.devices.reshape(DB, FB, XS, 2), ("y", "z", "x", "core"))
    owner, block = OWNER, ("y", "z")
    placed = (P(owner, block, None), P(owner, block, None, None), P(owner, None, None))
    return jax.shard_map(
        body, mesh=grid, in_specs=placed, out_specs=P(owner, block, None, None), check_vma=False
    )
```

time: 128 us -> 102 us (0.80)
  blocking collectives: 0 us -> 50.6 us
  waiting for transfers between devices: 40.5 us -> 5.29 us
  starting transfers between devices: 66.4 us -> 32.7 us
  local copies, waits for them, and re-layouts: 10.4 us -> 2.64 us
    all_to_all x0 -> x2, blocking collectives: none -> 50.6 us  [the longest x1 36.9 us: body(): lax.all_to_all(send, ('y', 'z'), split_axis=0, concat_axis=0, tiled=True)]
    all_to_all x3 -> x1, starting transfers between devices: 37.8 us -> 3.55 us  [body(): slots = lax.all_to_all(slots, 'y', split_axis=0, concat_axis=0, tiled=True)]
    all_to_all x3 -> x1, waiting for transfers between devices: 31.3 us -> 4.74 us  [body(): slots = lax.all_to_all(slots, 'y', split_axis=0, concat_axis=0, tiled=True)]
    ppermute x9 -> x8, waiting for transfers between devices: 9.16 us -> 0.55 us  [the longest x4 0.54 us: ahead(): return lax.ppermute(value, OWNER, pairs)]
    unnamed x19 -> x4, local copies, waits for them, and re-layouts: 5.33 us -> 0.93 us
    pallas_call x3 -> x4, Pallas kernels: 4.81 us -> 6.34 us  [the longest x1 4.28 us: body(): pl.pallas_call(product_kernel, out_shape=jax.ShapeDtypeStruct((OWN, DBLK,...]
    broadcast_in_dim x1 -> x0, local copies, waits for them, and re-layouts: 1.32 us -> none  [body(): jnp.broadcast_to(rest[None], (8, 2, SWAP - PART, TOK))]
    ppermute x9 -> x8, starting transfers between devices: 28.5 us -> 29.1 us  [the longest x4 15.9 us: ahead(): return lax.ppermute(value, OWNER, pairs)]
  transfers between devices with their start and end apart: 12 -> 9, of which waited for: 4 -> 2; matrix products, arithmetic and copies ran while one was open for 1% -> 0% of each run, Pallas kernels for 5% -> 5%
where the time goes in v3:
time: 102 us
  blocking collectives  50.6 us (50%)
  starting transfers between devices  32.7 us (32%)
  Pallas kernels  10 us (10%)
  waiting for transfers between devices  5.29 us (5%)
  local copies, waits for them, and re-layouts  2.64 us (3%)
    all_to_all x1, blocking collectives, body(): lax.all_to_all(send, ('y', 'z'), split_axis=0, concat_axis=0, tiled=True)  36.9 us
    ppermute x4, starting transfers between devices, ahead(): return lax.ppermute(value, OWNER, pairs)  15.9 us
    all_to_all x1, blocking collectives, body(): lax.all_to_all(routed, OWNER, split_axis=0, concat_axis=0, tiled=True)  13.7 us
    ppermute x4, starting transfers between devices, swap(): return lax.ppermute(value, 'core', [(0, 1), (1, 0)])  13.2 us
    all_to_all x1, waiting for transfers between devices, body(): slots = lax.all_to_all(slots, 'y', split_axis=0, concat_axis=0, tiled=True)  4.74 us
    pallas_call x1, Pallas kernels, body(): pl.pallas_call(product_kernel, out_shape=jax.ShapeDtypeStruct((OWN, DBLK,...  4.28 us
    all_to_all x1, starting transfers between devices, body(): slots = lax.all_to_all(slots, 'y', split_axis=0, concat_axis=0, tiled=True)  3.55 us
  transfers between devices with their start and end apart: 9, of which 2 were waited for; matrix products, arithmetic and copies ran while one was open for 0% of the time, Pallas kernels for 5%

profile of v3, /device:TPU:1, one launch (start us, length us, event | category | flops | bytes accessed | tf_op | source)
XLA Modules:
  0.0 101.7 jit_solution(1797898175684101879)
XLA Ops:
  0.0 1.1 %reshape_squeeze.7 = bf16[2,8,8,8,32]{4,3,2,1,0:T(8,128)(2,1)S(1)} reshape(bf16[1,2,8,2048]{3,2,1,0:T(8,128)(2,1)} %param.4) | data formatting | bytes 131072 | tf_op jit(solution)/shard_map/reshape;squeeze | solution.py:181
  1.1 0.2 copy.9
  1.3 0.2 concatenate.9
  1.4 0.8 copy.15
  2.2 0.1 broadcast_in_dim.4
  2.4 0.3 pad_maximum_fusion
  2.6 36.9 %all_to_all.15 = bf16[64,2,1152]{2,1,0:T(2,128)(2,1)S(1)} all-to-all(bf16[64,2,1152]{2,1,0:T(2,128)(2,1)S(1)} %pad_maximum_fusion), channel_id=1, replica_groups=mesh['y'=8,'z'=8,'x'=8,'core'=2] {'y','z'}, dimensions={0} | all-to-all | bytes 589824 | tf_op jit(solution)/shard_map/all_to_all | solution.py:184
  39.5 0.1 reshape.16
  39.7 0.2 copy.12
  39.9 5.0 %collective-permute-start = (bf16[896,128]{1,0:T(8,128)(2,1)S(1)}, bf16[896,128]{1,0:T(8,128)(2,1)S(1)}, u32[]{:S(2)}, u32[]{:S(2)}) collective-permute-start(bf16[896,128]{1,0:T(8,128)(2,1)S(1)} %bitcast.23), channel_id=1, source_target_pairs={{0,1},{1,0},{2,3},{3,2},{4,5},{5,4},{6,7},{7,6},{8,9},{9,8},{10,11... | collective-permute-start | bytes 688136 | tf_op jit(solution)/shard_map/ppermute | solution.py:167
  44.9 1.7 %shard_map.37.onehot_ref.after_ref = bf16[384,4096]{1,0:T(8,128)(2,1)S(1)} custom-call(s32[8,128]{1,0:T(8,128)S(1)} %bitcast.26), custom_call_target="tpu_custom_call" | custom-call | flops 4194304 | bytes 6291456 | tf_op jit(solution)/shard_map/pallas_call | solution.py:172
  46.6 0.0 collective-permute-done.other_ref
  46.7 5.4 %collective-permute-start.1 = (bf16[2,896,128]{2,1,0:T(8,128)(2,1)S(1)}, bf16[2,896,128]{2,1,0:T(8,128)(2,1)S(1)}, u32[]{:S(2)}, u32[]{:S(2)}) collective-permute-start(bf16[2,896,128]{2,1,0:T(8,128)(2,1)S(1)} %shard_map.39.refs_0_), channel_id=1, source_target_pairs={{0,4},{1,13},{2,6},{3,15},{4,8},{5,1},{6,10},{7,3},{8,12},{9,5},{1... | collective-permute-start | bytes 1376264 | tf_op jit(solution)/shard_map/ppermute | solution.py:163
  52.1 1.0 %shard_map.38 = bf16[16,32,128]{2,1,0:T(8,128)(2,1)S(1)} custom-call(bf16[128,256]{1,0:T(8,128)(2,1)S(1)} %slice.9.pieces_ref, bf16[384,4096]{1,0:T(8,128)(2,1)S(1)} %shard_map.37.onehot_ref.after_ref, s32[8,128]{1,0:T(8,128)S(1)} %bitcast.27), custom_call_target="tpu_custom_call" | custom-call | flops 536870912 | bytes 4194304 | tf_op jit(solution)/shard_map/pallas_call | solution.py:207
  53.1 13.7 %all_to_all.16.routed_ref = bf16[16,32,128]{2,1,0:T(8,128)(2,1)S(1)} all-to-all(bf16[16,32,128]{2,1,0:T(8,128)(2,1)S(1)} %shard_map.38), channel_id=1, replica_groups=mesh['y'=8,'z'=8,'x'=8,'core'=2] {'x','core'}, dimensions={0} | all-to-all | bytes 262144 | tf_op jit(solution)/shard_map/all_to_all | solution.py:214
  66.8 0.0 collective-permute-done.1.after_ref.refs_3_
  66.8 1.0 shard_map.40
  67.8 3.5 %all-to-all-start.2 = ((bf16[8,16,24,128]{3,2,1,0:T(8,128)(2,1)}), bf16[8,16,24,128]{3,2,1,0:T(8,128)(2,1)S(1)}, u32[]{:S(2)}, u32[]{:S(2)}) async-start(bf16[8,16,24,128]{3,2,1,0:T(8,128)(2,1)} %shard_map.40), calls=%async_computation.2 | async-start | bytes 1572864 | tf_op jit(solution)/shard_map/all_to_all | solution.py:225
  71.4 3.1 %collective-permute-start.2 = (bf16[2,896,128]{2,1,0:T(8,128)(2,1)S(1)}, bf16[2,896,128]{2,1,0:T(8,128)(2,1)S(1)}, u32[]{:S(2)}, u32[]{:S(2)}) collective-permute-start(bf16[2,896,128]{2,1,0:T(8,128)(2,1)S(1)} %shard_map.39.refs_0_), channel_id=1, source_target_pairs={{0,2},{1,15},{2,4},{3,1},{4,6},{5,3},{6,8},{7,5},{8,10},{9,7},{10,... | collective-permute-start | bytes 1376264 | tf_op jit(solution)/shard_map/ppermute | solution.py:163
  74.5 5.4 %collective-permute-start.5 = (bf16[2,896,128]{2,1,0:T(8,128)(2,1)S(1)}, bf16[2,896,128]{2,1,0:T(8,128)(2,1)S(1)}, u32[]{:S(2)}, u32[]{:S(2)}) collective-permute-start(bf16[2,896,128]{2,1,0:T(8,128)(2,1)S(1)} %collective-permute-done.1.after_ref.refs_3_), channel_id=1, source_target_pairs={{0,2},{1,15},{2,4},{3,1},{4,6},{5,3},{6,8},{7,5},{8,10},{9,7},{10,... | collective-permute-start | bytes 1376264 | tf_op jit(solution)/shard_map/ppermute | solution.py:163
  79.9 1.9 %collective-permute-start.4 = (bf16[2,896,128]{2,1,0:T(8,128)(2,1)S(1)}, bf16[2,896,128]{2,1,0:T(8,128)(2,1)S(1)}, u32[]{:S(2)}, u32[]{:S(2)}) collective-permute-start(bf16[2,896,128]{2,1,0:T(8,128)(2,1)S(1)} %collective-permute-done.1.after_ref.refs_3_), channel_id=1, source_target_pairs={{0,1},{1,0},{2,3},{3,2},{4,5},{5,4},{6,7},{7,6},{8,9},{9,8},{10,11... | collective-permute-start | bytes 1376264 | tf_op jit(solution)/shard_map/ppermute | solution.py:167
  81.9 2.0 %collective-permute-start.7 = (bf16[2,896,128]{2,1,0:T(8,128)(2,1)S(1)}, bf16[2,896,128]{2,1,0:T(8,128)(2,1)}, u32[]{:S(2)}, u32[]{:S(2)}) collective-permute-start(bf16[2,896,128]{2,1,0:T(8,128)(2,1)S(1)} %collective-permute-done.1.after_ref.refs_3_), channel_id=1, source_target_pairs={{0,4},{1,13},{2,6},{3,15},{4,8},{5,1},{6,10},{7,3},{8,12},{9,5},{1... | collective-permute-start | bytes 1376264 | tf_op jit(solution)/shard_map/ppermute | solution.py:163
  83.9 0.0 collective-permute-done.2.refs_1_
  83.9 3.1 %collective-permute-start.3 = (bf16[2,896,128]{2,1,0:T(8,128)(2,1)S(1)}, bf16[2,896,128]{2,1,0:T(8,128)(2,1)}, u32[]{:S(2)}, u32[]{:S(2)}) collective-permute-start(bf16[2,896,128]{2,1,0:T(8,128)(2,1)S(1)} %collective-permute-done.2.refs_1_), channel_id=1, source_target_pairs={{0,1},{1,0},{2,3},{3,2},{4,5},{5,4},{6,7},{7,6},{8,9},{9,8},{10,11... | collective-permute-start | bytes 1376264 | tf_op jit(solution)/shard_map/ppermute | solution.py:167
  87.0 0.0 collective-permute-done.5.refs_5_
  87.0 3.1 %collective-permute-start.6 = (bf16[2,896,128]{2,1,0:T(8,128)(2,1)S(1)}, bf16[2,896,128]{2,1,0:T(8,128)(2,1)}, u32[]{:S(2)}, u32[]{:S(2)}) collective-permute-start(bf16[2,896,128]{2,1,0:T(8,128)(2,1)S(1)} %collective-permute-done.5.refs_5_), channel_id=1, source_target_pairs={{0,1},{1,0},{2,3},{3,2},{4,5},{5,4},{6,7},{7,6},{8,9},{9,8},{10,11... | collective-permute-start | bytes 1376264 | tf_op jit(solution)/shard_map/ppermute | solution.py:167
  90.2 4.7 %all-to-all-done.2 = bf16[8,16,24,128]{3,2,1,0:T(8,128)(2,1)S(1)} async-done(((bf16[8,16,24,128]{3,2,1,0:T(8,128)(2,1)}), bf16[8,16,24,128]{3,2,1,0:T(8,128)(2,1)S(1)}, u32[]{:S(2)}, u32[]{:S(2)}) %all-to-all-start.2) | async-done | bytes 786464 | tf_op jit(solution)/shard_map/all_to_all | solution.py:225
  94.9 2.0 %shard_map.41.dense_ref = bf16[2048,512]{1,0:T(8,128)(2,1)S(1)} custom-call(s32[1]{0:T(128)} %bitcast.me_ref, bf16[16,32,128]{2,1,0:T(8,128)(2,1)S(1)} %all_to_all.16.routed_ref, bf16[8,384,128]{2,1,0:T(8,128)(2,1)S(1)} %bitcast.25), custom_call_target="tpu_custom_call" | custom-call | flops 1073741824 | bytes 4194304 | tf_op jit(solution)/shard_map/pallas_call | solution.py:228
  96.9 0.0 collective-permute-done.4.refs_4_
  96.9 0.5 collective-permute-done.7.refs_7_
  97.4 0.0 collective-permute-done.3.refs_2_
  97.4 4.3 %shard_map.42 = bf16[2,896,256]{2,1,0:T(8,128)(2,1)} custom-call(bf16[2048,512]{1,0:T(8,128)(2,1)S(1)} %shard_map.41.dense_ref, bf16[2,896,128]{2,1,0:T(8,128)(2,1)S(1)} %shard_map.39.refs_0_, bf16[2,896,128]{2,1,0:T(8,128)(2,1)S(1)} %collective-permute-done.2.refs_1_, bf16[2,896,128]{2,1,0:T(8,128)(2,1)} %collective-permute-done.3.refs_2_, ...), custom_call_target="tpu_custom_call" | custom-call | flops 1879048192 | bytes 7340032 | tf_op jit(solution)/shard_map/pallas_call | solution.py:242
  (7 shorter events, 0.1 us)
Async XLA Ops:
  0.0 44.9 %copy-start = (s32[1,128,8]{1,2,0:T(8,128)S(1)}, s32[1,128,8]{1,2,0:T(8,128)}, u32[]{:S(2)}) copy-start(s32[1,128,8]{1,2,0:T(8,128)} %param.5) | copy-start | bytes 12292
  39.9 6.8 %collective-permute-start = (bf16[896,128]{1,0:T(8,128)(2,1)S(1)}, bf16[896,128]{1,0:T(8,128)(2,1)S(1)}, u32[]{:S(2)}, u32[]{:S(2)}) collective-permute-start(bf16[896,128]{1,0:T(8,128)(2,1)S(1)} %bitcast.23), channel_id=1, source_target_pairs={{0,1},{1,0},{2,3},{3,2},{4,5},{5,4},{6,7},{7,6},{8,9},{9,8},{10,11... | collective-permute-start | bytes 688136 | tf_op jit(solution)/shard_map/ppermute | solution.py:167
  46.7 20.1 %collective-permute-start.1 = (bf16[2,896,128]{2,1,0:T(8,128)(2,1)S(1)}, bf16[2,896,128]{2,1,0:T(8,128)(2,1)S(1)}, u32[]{:S(2)}, u32[]{:S(2)}) collective-permute-start(bf16[2,896,128]{2,1,0:T(8,128)(2,1)S(1)} %shard_map.39.refs_0_), channel_id=1, source_target_pairs={{0,4},{1,13},{2,6},{3,15},{4,8},{5,1},{6,10},{7,3},{8,12},{9,5},{1... | collective-permute-start | bytes 1376264 | tf_op jit(solution)/shard_map/ppermute | solution.py:163
  67.8 27.1 %all-to-all-start.2 = ((bf16[8,16,24,128]{3,2,1,0:T(8,128)(2,1)}), bf16[8,16,24,128]{3,2,1,0:T(8,128)(2,1)S(1)}, u32[]{:S(2)}, u32[]{:S(2)}) async-start(bf16[8,16,24,128]{3,2,1,0:T(8,128)(2,1)} %shard_map.40), calls=%async_computation.2 | async-start | bytes 1572864 | tf_op jit(solution)/shard_map/all_to_all | solution.py:225
  71.4 12.5 %collective-permute-start.2 = (bf16[2,896,128]{2,1,0:T(8,128)(2,1)S(1)}, bf16[2,896,128]{2,1,0:T(8,128)(2,1)S(1)}, u32[]{:S(2)}, u32[]{:S(2)}) collective-permute-start(bf16[2,896,128]{2,1,0:T(8,128)(2,1)S(1)} %shard_map.39.refs_0_), channel_id=1, source_target_pairs={{0,2},{1,15},{2,4},{3,1},{4,6},{5,3},{6,8},{7,5},{8,10},{9,7},{10,... | collective-permute-start | bytes 1376264 | tf_op jit(solution)/shard_map/ppermute | solution.py:163
  74.5 12.5 %collective-permute-start.5 = (bf16[2,896,128]{2,1,0:T(8,128)(2,1)S(1)}, bf16[2,896,128]{2,1,0:T(8,128)(2,1)S(1)}, u32[]{:S(2)}, u32[]{:S(2)}) collective-permute-start(bf16[2,896,128]{2,1,0:T(8,128)(2,1)S(1)} %collective-permute-done.1.after_ref.refs_3_), channel_id=1, source_target_pairs={{0,2},{1,15},{2,4},{3,1},{4,6},{5,3},{6,8},{7,5},{8,10},{9,7},{10,... | collective-permute-start | bytes 1376264 | tf_op jit(solution)/shard_map/ppermute | solution.py:163
  79.9 17.0 %collective-permute-start.4 = (bf16[2,896,128]{2,1,0:T(8,128)(2,1)S(1)}, bf16[2,896,128]{2,1,0:T(8,128)(2,1)S(1)}, u32[]{:S(2)}, u32[]{:S(2)}) collective-permute-start(bf16[2,896,128]{2,1,0:T(8,128)(2,1)S(1)} %collective-permute-done.1.after_ref.refs_3_), channel_id=1, source_target_pairs={{0,1},{1,0},{2,3},{3,2},{4,5},{5,4},{6,7},{7,6},{8,9},{9,8},{10,11... | collective-permute-start | bytes 1376264 | tf_op jit(solution)/shard_map/ppermute | solution.py:167
  81.9 15.6 %collective-permute-start.7 = (bf16[2,896,128]{2,1,0:T(8,128)(2,1)S(1)}, bf16[2,896,128]{2,1,0:T(8,128)(2,1)}, u32[]{:S(2)}, u32[]{:S(2)}) collective-permute-start(bf16[2,896,128]{2,1,0:T(8,128)(2,1)S(1)} %collective-permute-done.1.after_ref.refs_3_), channel_id=1, source_target_pairs={{0,4},{1,13},{2,6},{3,15},{4,8},{5,1},{6,10},{7,3},{8,12},{9,5},{1... | collective-permute-start | bytes 1376264 | tf_op jit(solution)/shard_map/ppermute | solution.py:163
  83.9 13.5 %collective-permute-start.3 = (bf16[2,896,128]{2,1,0:T(8,128)(2,1)S(1)}, bf16[2,896,128]{2,1,0:T(8,128)(2,1)}, u32[]{:S(2)}, u32[]{:S(2)}) collective-permute-start(bf16[2,896,128]{2,1,0:T(8,128)(2,1)S(1)} %collective-permute-done.2.refs_1_), channel_id=1, source_target_pairs={{0,1},{1,0},{2,3},{3,2},{4,5},{5,4},{6,7},{7,6},{8,9},{9,8},{10,11... | collective-permute-start | bytes 1376264 | tf_op jit(solution)/shard_map/ppermute | solution.py:167
  87.0 10.4 %collective-permute-start.6 = (bf16[2,896,128]{2,1,0:T(8,128)(2,1)S(1)}, bf16[2,896,128]{2,1,0:T(8,128)(2,1)}, u32[]{:S(2)}, u32[]{:S(2)}) collective-permute-start(bf16[2,896,128]{2,1,0:T(8,128)(2,1)S(1)} %collective-permute-done.5.refs_5_), channel_id=1, source_target_pairs={{0,1},{1,0},{2,3},{3,2},{4,5},{5,4},{6,7},{7,6},{8,9},{9,8},{10,11... | collective-permute-start | bytes 1376264 | tf_op jit(solution)/shard_map/ppermute | solution.py:167

commit v4 on v3

--- a/solution.py
+++ b/solution.py
@@ -18,6 +18,9 @@
 OWNERS = 16
 HALF = CAP // 2
 LANES = 128
+FIRST = 5
+PAIRS = 8
+ROOM = 64
 XS = 8
 OWNER = ("x", "core")
 
@@ -75,6 +78,29 @@
             slots_ref[y, g] = slots
 
 
+def send_kernel(tokens_ref, grads_ref, out_ref):
+    for y in range(DB):
+        block = tokens_ref[:, y * DBLK : (y + 1) * DBLK]
+        for z in range(FB):
+            out_ref[y * FB + z, :, :DBLK] = block
+    lane = lax.broadcasted_iota(jnp.int32, (TOP, FBLK), 1)
+    row = lax.broadcasted_iota(jnp.int32, (TOP, FBLK), 0)
+    turn = (lane // PIECE + DB - row) % DB
+    for z in range(FB):
+        turned = []
+        for i in range(2):
+            block = grads_ref[i, :, z * FBLK : (z + 1) * FBLK].astype(jnp.float32)
+            value = block
+            for by in range(1, DB):
+                moved = pltpu.roll(pltpu.roll(block, by * PIECE, 1), DB - by, 0)
+                value = jnp.where(turn == by, moved, value)
+            turned.append(value)
+        for y in range(DB):
+            out_ref[y * FB + z, :, DBLK:] = jnp.concatenate(
+                [value[y : y + 1] for value in turned], axis=0
+            ).astype(jnp.bfloat16)
+
+
 def both_kernel(mine_ref, other_ref, after_ref, out_ref):
     del after_ref
     out_ref[0] = mine_ref[...]
@@ -88,10 +114,10 @@
     for away, first in (
         (0, core),
         (-1, core),
-        (1, 1 - core),
         (-2, core),
         (2, 1 - core),
         (-3, core),
+        (1, 1 - core),
         (3, 1 - core),
         (4, core),
     ):
@@ -100,52 +126,97 @@
     return order
 
 
-def dense_kernel(me_ref, routed_ref, slots_ref, dense_ref, value_ref):
-    source = lax.broadcasted_iota(jnp.int32, (DB * LANES, FBLK), 0)
-    column = lax.broadcasted_iota(jnp.int32, (DB * LANES, FBLK), 1)
-    lane = source % LANES
-    wanted = (source // LANES) * PIECE + lane % PIECE
-    slots = jnp.concatenate([slots_ref[y] for y in range(DB)], axis=1)
-    spread = []
-    for j in range(4):
-        pick = ((column == wanted) & (lane // PIECE == j)).astype(jnp.bfloat16)
-        spread.append(jnp.dot(slots, pick, preferred_element_type=jnp.float32))
-    for e in range(OWN):
-        for g in range(OWNERS):
-            rows = slice(g * HALF, (g + 1) * HALF)
-            value_ref[e, g] = jnp.concatenate(
-                [spread[2 * e][rows], spread[2 * e + 1][rows]], axis=0
-            ).astype(jnp.bfloat16)
+def pair_rows(ref):
+    return jnp.concatenate([ref[0], ref[1]], axis=1)
+
+
+def early_kernel(me_ref, routed_ref, *refs):
+    parts, out_ref = refs[:FIRST], refs[-1]
     order = group_order(me_ref[0])
     named = []
-    for e in range(OWN):
-        for i in range(OWNERS):
-            ids = routed_ref[order[i]].astype(jnp.float32)[HALF:].astype(jnp.int32)
+    for i in range(OWNERS):
+        ids = routed_ref[order[i]].astype(jnp.float32)[HALF:].astype(jnp.int32)
+        for e in range(OWN):
             hit = (ids == OWN * me_ref[0] + e).astype(jnp.float32)
             named.append(jnp.sum(hit, axis=0, keepdims=True))
     named = jnp.concatenate(named, axis=0)
     before = jnp.dot(named.astype(jnp.bfloat16), earlier(), preferred_element_type=jnp.float32)
     place = jnp.where(named > 0.0, before, -1.0).T
-    number = lax.broadcasted_iota(jnp.int32, (TOK, CAP), 1).astype(jnp.float32)
+    lane = lax.broadcasted_iota(jnp.int32, (TOK, 4 * ROOM), 1)
+    number = (lane % ROOM).astype(jnp.float32)
+    for p in range(PAIRS):
+        halves = []
+        for h in range(2):
+            at = 2 * (2 * p + h)
+            slot = jnp.where(lane < 2 * ROOM, place[:, at : at + 1], place[:, at + 1 : at + 2])
+            mine = (slot == number) & ((lane // ROOM) % 2 == h)
+            halves.append(mine.astype(jnp.bfloat16))
+        pick = jnp.concatenate(halves, axis=0)
+        if p < FIRST:
+            out_ref[p * DBLK : (p + 1) * DBLK, :] = jnp.dot(
+                pair_rows(parts[p]), pick, preferred_element_type=jnp.float32
+            ).astype(jnp.bfloat16)
+        else:
+            at = FIRST * DBLK + (p - FIRST) * 2 * TOK
+            out_ref[at : at + 2 * TOK, :] = pick
+
+
+def value_kernel(slots_ref, value_ref):
+    rows = OWNERS * HALF
+    halves = []
+    for h in range(2):
+        halves.append(jnp.concatenate([slots_ref[4 * h + b] for b in range(4)], axis=1))
+    row = lax.broadcasted_iota(jnp.int32, (4 * LANES, 4 * LANES), 0)
+    col = lax.broadcasted_iota(jnp.int32, (4 * LANES, 4 * LANES), 1)
+    same = row % PIECE + (row // LANES) * PIECE == col % LANES
+    spread = (same & ((row % LANES) // PIECE == col // LANES)).astype(jnp.bfloat16)
+    spread = jnp.dot(
+        jnp.concatenate(halves, axis=0), spread, preferred_element_type=jnp.float32
+    )
+    empty = jnp.zeros((ROOM - CAP, FBLK), jnp.float32)
     for e in range(OWN):
-        for i in range(OWNERS):
-            at = e * OWNERS + i
-            pick = (place[:, at : at + 1] == number).astype(jnp.bfloat16)
-            dense_ref[i * TOK : (i + 1) * TOK, e * FBLK : (e + 1) * FBLK] = jnp.dot(
-                pick, value_ref[e, order[i]], preferred_element_type=jnp.float32
+        for g in range(OWNERS):
+            value = []
+            for j in (2 * e, 2 * e + 1):
+                lanes = slice(j * LANES, (j + 1) * LANES)
+                left = spread[g * HALF : (g + 1) * HALF, lanes]
+                right = spread[rows + g * HALF : rows + (g + 1) * HALF, lanes]
+                value.append(jnp.concatenate([left, right], axis=1))
+            value_ref[e, g] = jnp.concatenate(value + [empty], axis=0).astype(jnp.bfloat16)
+
+
+def sums(packed, value_ref, order, e):
+    lanes = slice(2 * e * ROOM, 2 * (e + 1) * ROOM)
+    left = jnp.concatenate([value[:, lanes] for value in packed], axis=1)
+    right = jnp.concatenate([value_ref[e, g] for g in order], axis=0)
+    return jnp.dot(left, right, preferred_element_type=jnp.float32)
+
+
+def first_kernel(me_ref, value_ref, early_ref, total_ref, right_ref):
+    order = group_order(me_ref[0])[: 2 * FIRST]
+    packed = [early_ref[p * DBLK : (p + 1) * DBLK, :] for p in range(FIRST)]
+    for e in range(OWN):
+        for i, g in enumerate(order):
+            right_ref[e, i * ROOM : (i + 1) * ROOM, :] = value_ref[e, g]
+    for e in range(OWN):
+        lanes = slice(2 * e * ROOM, 2 * (e + 1) * ROOM)
+        left = jnp.concatenate([value[:, lanes] for value in packed], axis=1)
+        total_ref[e] = jnp.dot(left, right_ref[e], preferred_element_type=jnp.float32)
+
+
+def last_kernel(me_ref, value_ref, early_ref, total_ref, *refs):
+    out_ref = refs[-1]
+    order = group_order(me_ref[0])[2 * FIRST :]
+    packed = []
+    for p in range(PAIRS - FIRST):
+        at = FIRST * DBLK + p * 2 * TOK
+        packed.append(
+            jnp.dot(
+                pair_rows(refs[p]), early_ref[at : at + 2 * TOK, :], preferred_element_type=jnp.float32
             ).astype(jnp.bfloat16)
-
-
-def product_kernel(dense_ref, *refs):
-    out_ref = refs[-1]
-    left = []
-    for ref in refs[:-1]:
-        left += [ref[i] for i in range(ref.shape[0])]
-    total = jnp.dot(
-        jnp.concatenate(left, axis=1), dense_ref[...], preferred_element_type=jnp.float32
-    )
+        )
     for e in range(OWN):
-        out_ref[e] = total[:, e * FBLK : (e + 1) * FBLK].astype(jnp.bfloat16)
+        out_ref[e] = (total_ref[e] + sums(packed, value_ref, order, e)).astype(jnp.bfloat16)
 
 
 def params(mib):
@@ -176,11 +247,12 @@
         compiler_params=params(16),
     )(ids)
 
-    x_part = tokens[0].reshape(2, DB, DBLK).transpose(1, 0, 2)
-    x_part = jnp.broadcast_to(x_part[:, None], (DB, FB, 2, DBLK))
-    g_part = slot_grads[0].reshape(2, TOP, FB, DB, PIECE).transpose(3, 2, 0, 1, 4)
-    g_part = g_part.reshape(DB, FB, 2, TOP * PIECE)
-    send = jnp.concatenate([x_part, g_part], axis=3).reshape(DB * FB, 2, DBLK + FBLK)
+    send = pl.pallas_call(
+        send_kernel,
+        out_shape=jax.ShapeDtypeStruct((DB * FB, 2, DBLK + FBLK), jnp.bfloat16),
+        cost_estimate=cost(1 << 31, 1 << 19),
+        compiler_params=params(16),
+    )(tokens[0], slot_grads[0])
     got = lax.all_to_all(send, ("y", "z"), split_axis=0, concat_axis=0, tiled=True)
     got = got.reshape(TOK, DBLK + FBLK)
 
@@ -225,26 +297,37 @@
     slots = lax.all_to_all(slots, "y", split_axis=0, concat_axis=0, tiled=True)
 
     me = lax.axis_index(OWNER).astype(jnp.int32).reshape(1)
-    dense = pl.pallas_call(
-        dense_kernel,
-        in_specs=[
-            pl.BlockSpec(memory_space=pltpu.SMEM),
-            pl.BlockSpec(memory_space=pltpu.VMEM),
-            pl.BlockSpec(memory_space=pltpu.VMEM),
-        ],
-        out_shape=jax.ShapeDtypeStruct((OWNERS * TOK, OWN * FBLK), jnp.bfloat16),
-        scratch_shapes=[pltpu.VMEM((OWN, OWNERS, CAP, FBLK), jnp.bfloat16)],
+    scalar, vmem = pl.BlockSpec(memory_space=pltpu.SMEM), pl.BlockSpec(memory_space=pltpu.VMEM)
+    early = pl.pallas_call(
+        early_kernel,
+        in_specs=[scalar] + [vmem] * (1 + FIRST),
+        out_shape=jax.ShapeDtypeStruct(
+            (FIRST * DBLK + (PAIRS - FIRST) * 2 * TOK, 4 * ROOM), jnp.bfloat16
+        ),
         cost_estimate=cost(1 << 30, 4 << 20),
-        compiler_params=params(16),
-    )(me, routed, slots.reshape(DB, OWNERS * HALF, LANES))
-
-    parts = [here, near, swap(near), next_, swap(next_), third, swap(third), far]
+        compiler_params=params(60),
+    )(me, routed, here, near, next_, swap(next_), third)
+    value = pl.pallas_call(
+        value_kernel,
+        out_shape=jax.ShapeDtypeStruct((OWN, OWNERS, ROOM, FBLK), jnp.bfloat16),
+        cost_estimate=cost(1 << 32, 2 << 20),
+        compiler_params=params(12),
+    )(slots.reshape(DB, OWNERS * HALF, LANES))
+    total = pl.pallas_call(
+        first_kernel,
+        in_specs=[scalar, vmem, vmem],
+        out_shape=jax.ShapeDtypeStruct((OWN, DBLK, FBLK), jnp.float32),
+        scratch_shapes=[pltpu.VMEM((OWN, 2 * FIRST * ROOM, FBLK), jnp.bfloat16)],
+        cost_estimate=cost(1 << 30, 4 << 20),
+        compiler_params=params(16),
+    )(me, value, early)
     out = pl.pallas_call(
-        product_kernel,
+        last_kernel,
+        in_specs=[scalar] + [vmem] * (3 + PAIRS - FIRST),
         out_shape=jax.ShapeDtypeStruct((OWN, DBLK, FBLK), jnp.bfloat16),
-        cost_estimate=cost(2 * DBLK * 2048 * 512, 7 << 20),
-        compiler_params=params(24),
-    )(dense, *parts)
+        cost_estimate=cost(1 << 30, 5 << 20),
+        compiler_params=params(16),
+    )(me, value, early, total, swap(near), swap(third), far)
     return out[:, None]
 
 

time: 102 us -> 99.7 us (0.977)
  waiting for transfers between devices: 5.29 us -> 0.37 us
  Pallas kernels: 10 us -> 11.9 us
    all_to_all x1, waiting for transfers between devices: 4.74 us -> 0.35 us  [body(): slots = lax.all_to_all(slots, 'y', split_axis=0, concat_axis=0, tiled=True)]
    unnamed x4 -> x17, local copies, waits for them, and re-layouts: 0.93 us -> 2.92 us
    pallas_call x2 -> x5, Pallas kernels: 6.26 us -> 8.01 us  [the longest x1 4.35 us: body(): pl.pallas_call(early_kernel, in_specs=[scalar] + [vmem] * (1 + FIRST), ou...]
    another operation x1 -> x0, local copies, waits for them, and re-layouts: 1.08 us -> none  [body(): slot_grads[0].reshape(2, TOP, FB, DB, PIECE).transpose(3, 2, 0, 1, 4)]
  transfers between devices with their start and end apart: 9 -> 9, of which waited for: 2 -> 1; matrix products, arithmetic and copies ran while one was open for 0% -> 0% of each run, Pallas kernels for 5% -> 9%
where the time goes in v4:
time: 99.7 us; the launch traced here: 98.8 us
  blocking collectives  50.6 us (51%)
  starting transfers between devices  32.7 us (33%)
  Pallas kernels  11.9 us (12%)
  local copies, waits for them, and re-layouts  3.06 us (3%)
    all_to_all x1, blocking collectives, body(): lax.all_to_all(send, ('y', 'z'), split_axis=0, concat_axis=0, tiled=True)  36.9 us
    ppermute x4, starting transfers between devices, ahead(): return lax.ppermute(value, OWNER, pairs)  15.9 us
    all_to_all x1, blocking collectives, body(): lax.all_to_all(routed, OWNER, split_axis=0, concat_axis=0, tiled=True)  13.7 us
    ppermute x4, starting transfers between devices, swap(): return lax.ppermute(value, 'core', [(0, 1), (1, 0)])  13.2 us
    pallas_call x1, Pallas kernels, body(): pl.pallas_call(early_kernel, in_specs=[scalar] + [vmem] * (1 + FIRST), ou...  4.35 us
    all_to_all x1, starting transfers between devices, body(): slots = lax.all_to_all(slots, 'y', split_axis=0, concat_axis=0, tiled=True)  3.55 us
    unnamed x17, local copies, waits for them, and re-layouts  2.92 us
  transfers between devices with their start and end apart: 9, of which 1 were waited for; matrix products, arithmetic and copies ran while one was open for 0% of the time, Pallas kernels for 9%

profile of v4, /device:TPU:1, one launch (start us, length us, event | category | flops | bytes accessed | tf_op | source)
XLA Modules:
  0.0 98.8 jit_solution(7092932524923864623)
XLA Ops:
  0.0 0.8 copy-done.5
  0.8 0.7 copy-done.6
  1.6 0.2 shard_map.37
  1.8 36.9 %all_to_all.15 = bf16[64,2,1152]{2,1,0:T(2,128)(2,1)S(1)} all-to-all(bf16[64,2,1152]{2,1,0:T(2,128)(2,1)S(1)} %shard_map.37), channel_id=1, replica_groups=mesh['y'=8,'z'=8,'x'=8,'core'=2] {'y','z'}, dimensions={0} | all-to-all | bytes 589824 | tf_op jit(solution)/shard_map/all_to_all | solution.py:256
  38.8 0.1 reshape.10
  38.9 0.2 copy.9
  39.1 5.0 %collective-permute-start = (bf16[896,128]{1,0:T(8,128)(2,1)S(1)}, bf16[896,128]{1,0:T(8,128)(2,1)S(1)}, u32[]{:S(2)}, u32[]{:S(2)}) collective-permute-start(bf16[896,128]{1,0:T(8,128)(2,1)S(1)} %bitcast.11), channel_id=1, source_target_pairs={{0,1},{1,0},{2,3},{3,2},{4,5},{5,4},{6,7},{7,6},{8,9},{9,8},{10,11... | collective-permute-start | bytes 688136 | tf_op jit(solution)/shard_map/ppermute | solution.py:238
  44.1 1.7 %shard_map.38.onehot_ref.after_ref = bf16[384,4096]{1,0:T(8,128)(2,1)S(1)} custom-call(s32[8,128]{1,0:T(8,128)S(1)} %bitcast.14), custom_call_target="tpu_custom_call" | custom-call | flops 4194304 | bytes 6291456 | tf_op jit(solution)/shard_map/pallas_call | solution.py:243
  45.8 0.0 collective-permute-done.other_ref
  45.9 5.4 %collective-permute-start.1 = (bf16[2,896,128]{2,1,0:T(8,128)(2,1)S(1)}, bf16[2,896,128]{2,1,0:T(8,128)(2,1)S(1)}, u32[]{:S(2)}, u32[]{:S(2)}) collective-permute-start(bf16[2,896,128]{2,1,0:T(8,128)(2,1)S(1)} %shard_map.40.refs_0_), channel_id=1, source_target_pairs={{0,4},{1,13},{2,6},{3,15},{4,8},{5,1},{6,10},{7,3},{8,12},{9,5},{1... | collective-permute-start | bytes 1376264 | tf_op jit(solution)/shard_map/ppermute | solution.py:234
  51.3 1.0 %shard_map.39 = bf16[16,32,128]{2,1,0:T(8,128)(2,1)S(1)} custom-call(bf16[128,256]{1,0:T(8,128)(2,1)S(1)} %slice.9.pieces_ref, bf16[384,4096]{1,0:T(8,128)(2,1)S(1)} %shard_map.38.onehot_ref.after_ref, s32[8,128]{1,0:T(8,128)S(1)} %bitcast.15), custom_call_target="tpu_custom_call" | custom-call | flops 536870912 | bytes 4194304 | tf_op jit(solution)/shard_map/pallas_call | solution.py:279
  52.3 13.7 %all_to_all.16.routed_ref = bf16[16,32,128]{2,1,0:T(8,128)(2,1)S(1)} all-to-all(bf16[16,32,128]{2,1,0:T(8,128)(2,1)S(1)} %shard_map.39), channel_id=1, replica_groups=mesh['y'=8,'z'=8,'x'=8,'core'=2] {'x','core'}, dimensions={0} | all-to-all | bytes 262144 | tf_op jit(solution)/shard_map/all_to_all | solution.py:286
  66.0 0.0 collective-permute-done.1.after_ref.refs_2_
  66.0 1.1 %shard_map.41 = bf16[8,16,24,128]{3,2,1,0:T(8,128)(2,1)} custom-call(bf16[16,32,128]{2,1,0:T(8,128)(2,1)S(1)} %all_to_all.16.routed_ref, bf16[2,896,128]{2,1,0:T(8,128)(2,1)S(1)} %collective-permute-done.1.after_ref.refs_2_), custom_call_target="tpu_custom_call" | custom-call | flops 1048576 | bytes 1048576 | tf_op jit(solution)/shard_map/pallas_call | solution.py:287
  67.1 3.5 %all-to-all-start.2 = ((bf16[8,16,24,128]{3,2,1,0:T(8,128)(2,1)}), bf16[8,16,24,128]{3,2,1,0:T(8,128)(2,1)S(1)}, u32[]{:S(2)}, u32[]{:S(2)}) async-start(bf16[8,16,24,128]{3,2,1,0:T(8,128)(2,1)} %shard_map.41), calls=%async_computation.2 | async-start | bytes 1572864 | tf_op jit(solution)/shard_map/all_to_all | solution.py:297
  70.7 3.1 %collective-permute-start.2 = (bf16[2,896,128]{2,1,0:T(8,128)(2,1)S(1)}, bf16[2,896,128]{2,1,0:T(8,128)(2,1)}, u32[]{:S(2)}, u32[]{:S(2)}) collective-permute-start(bf16[2,896,128]{2,1,0:T(8,128)(2,1)S(1)} %shard_map.40.refs_0_), channel_id=1, source_target_pairs={{0,2},{1,15},{2,4},{3,1},{4,6},{5,3},{6,8},{7,5},{8,10},{9,7},{10,... | collective-permute-start | bytes 1376264 | tf_op jit(solution)/shard_map/ppermute | solution.py:234
  73.8 5.4 %collective-permute-start.4 = (bf16[2,896,128]{2,1,0:T(8,128)(2,1)S(1)}, bf16[2,896,128]{2,1,0:T(8,128)(2,1)S(1)}, u32[]{:S(2)}, u32[]{:S(2)}) collective-permute-start(bf16[2,896,128]{2,1,0:T(8,128)(2,1)S(1)} %collective-permute-done.1.after_ref.refs_2_), channel_id=1, source_target_pairs={{0,2},{1,15},{2,4},{3,1},{4,6},{5,3},{6,8},{7,5},{8,10},{9,7},{10,... | collective-permute-start | bytes 1376264 | tf_op jit(solution)/shard_map/ppermute | solution.py:234
  79.3 1.9 %collective-permute-start.3 = (bf16[2,896,128]{2,1,0:T(8,128)(2,1)S(1)}, bf16[2,896,128]{2,1,0:T(8,128)(2,1)}, u32[]{:S(2)}, u32[]{:S(2)}) collective-permute-start(bf16[2,896,128]{2,1,0:T(8,128)(2,1)S(1)} %collective-permute-done.1.after_ref.refs_2_), channel_id=1, source_target_pairs={{0,1},{1,0},{2,3},{3,2},{4,5},{5,4},{6,7},{7,6},{8,9},{9,8},{10,11... | collective-permute-start | bytes 1376264 | tf_op jit(solution)/shard_map/ppermute | solution.py:238
  81.2 2.0 %collective-permute-start.7 = (bf16[2,896,128]{2,1,0:T(8,128)(2,1)S(1)}, bf16[2,896,128]{2,1,0:T(8,128)(2,1)S(1)}, u32[]{:S(2)}, u32[]{:S(2)}) collective-permute-start(bf16[2,896,128]{2,1,0:T(8,128)(2,1)S(1)} %collective-permute-done.1.after_ref.refs_2_), channel_id=1, source_target_pairs={{0,4},{1,13},{2,6},{3,15},{4,8},{5,1},{6,10},{7,3},{8,12},{9,5},{1... | collective-permute-start | bytes 1376264 | tf_op jit(solution)/shard_map/ppermute | solution.py:234
  83.2 0.0 collective-permute-done.2.refs_1_
  83.2 3.1 %collective-permute-start.5 = (bf16[2,896,128]{2,1,0:T(8,128)(2,1)}, bf16[2,896,128]{2,1,0:T(8,128)(2,1)S(1)}, u32[]{:S(2)}, u32[]{:S(2)}) collective-permute-start(bf16[2,896,128]{2,1,0:T(8,128)(2,1)} %collective-permute-done.2.refs_1_), channel_id=1, source_target_pairs={{0,1},{1,0},{2,3},{3,2},{4,5},{5,4},{6,7},{7,6},{8,9},{9,8},{10,11... | collective-permute-start | bytes 1376264 | tf_op jit(solution)/shard_map/ppermute | solution.py:238
  86.3 0.0 collective-permute-done.4.refs_4_
  86.3 3.1 %collective-permute-start.6 = (bf16[2,896,128]{2,1,0:T(8,128)(2,1)S(1)}, bf16[2,896,128]{2,1,0:T(8,128)(2,1)S(1)}, u32[]{:S(2)}, u32[]{:S(2)}) collective-permute-start(bf16[2,896,128]{2,1,0:T(8,128)(2,1)S(1)} %collective-permute-done.4.refs_4_), channel_id=1, source_target_pairs={{0,1},{1,0},{2,3},{3,2},{4,5},{5,4},{6,7},{7,6},{8,9},{9,8},{10,11... | collective-permute-start | bytes 1376264 | tf_op jit(solution)/shard_map/ppermute | solution.py:238
  89.5 0.0 collective-permute-done.3.refs_3_
  89.5 4.3 %shard_map.43.early_ref = bf16[5248,256]{1,0:T(8,128)(2,1)} custom-call(s32[1]{0:T(128)} %bitcast.me_ref, bf16[16,32,128]{2,1,0:T(8,128)(2,1)} %copy-done.3, bf16[2,896,128]{2,1,0:T(8,128)(2,1)} %copy-done.2, bf16[2,896,128]{2,1,0:T(8,128)(2,1)} %collective-permute-done.2.refs_1_, bf16[2,896,128]{2,1,0:T(8,128)(2,1)} %copy-done.1, ...), custom_call_target="tpu_custom_call" | custom-call | flops 1073741824 | bytes 4194304 | tf_op jit(solution)/shard_map/pallas_call | solution.py:301
  93.9 0.3 all-to-all-done.2
  94.2 0.6 shard_map.42.value_ref
  94.8 1.1 %copy-done = bf16[5248,256]{1,0:T(8,128)(2,1)S(1)} copy-done((bf16[5248,256]{1,0:T(8,128)(2,1)S(1)}, bf16[5248,256]{1,0:T(8,128)(2,1)}, u32[]{:S(2)}) %copy-start) | copy-done | bytes 2687000
  96.0 0.9 shard_map.44.total_ref
  96.9 0.0 collective-permute-done.5.refs_0_
  96.9 0.0 collective-permute-done.7.refs_2_
  96.9 1.9 %shard_map.45 = bf16[2,896,256]{2,1,0:T(8,128)(2,1)} custom-call(s32[1]{0:T(128)} %bitcast.me_ref, bf16[2,16,64,256]{3,2,1,0:T(8,128)(2,1)S(1)} %shard_map.42.value_ref, bf16[5248,256]{1,0:T(8,128)(2,1)S(1)} %copy-done, f32[2,896,256]{2,1,0:T(8,128)S(1)} %shard_map.44.total_ref, bf16[2,896,128]{2,1,0:T(8,128)(2,1)S(1)} %collective-permute-done.5.refs_0_, ...), custom_call_target="tpu_custom_call" | custom-call | flops 1073741824 | bytes 5242880 | tf_op jit(solution)/shard_map/pallas_call | solution.py:324
  (17 shorter events, 0.1 us)
Async XLA Ops:
  0.0 0.8 copy-start.5
  0.8 0.7 copy-start.6
  1.6 42.6 %copy-start.4 = (s32[1,128,8]{1,2,0:T(8,128)S(1)}, s32[1,128,8]{1,2,0:T(8,128)}, u32[]{:S(2)}) copy-start(s32[1,128,8]{1,2,0:T(8,128)} %param.5) | copy-start | bytes 12292
  39.1 6.8 %collective-permute-start = (bf16[896,128]{1,0:T(8,128)(2,1)S(1)}, bf16[896,128]{1,0:T(8,128)(2,1)S(1)}, u32[]{:S(2)}, u32[]{:S(2)}) collective-permute-start(bf16[896,128]{1,0:T(8,128)(2,1)S(1)} %bitcast.11), channel_id=1, source_target_pairs={{0,1},{1,0},{2,3},{3,2},{4,5},{5,4},{6,7},{7,6},{8,9},{9,8},{10,11... | collective-permute-start | bytes 688136 | tf_op jit(solution)/shard_map/ppermute | solution.py:238
  45.9 24.8 %copy-start.2 = (bf16[2,896,128]{2,1,0:T(8,128)(2,1)}, bf16[2,896,128]{2,1,0:T(8,128)(2,1)S(1)}, u32[]{:S(2)}) copy-start(bf16[2,896,128]{2,1,0:T(8,128)(2,1)S(1)} %shard_map.40.refs_0_) | copy-start | bytes 1376260
  45.9 20.1 %collective-permute-start.1 = (bf16[2,896,128]{2,1,0:T(8,128)(2,1)S(1)}, bf16[2,896,128]{2,1,0:T(8,128)(2,1)S(1)}, u32[]{:S(2)}, u32[]{:S(2)}) collective-permute-start(bf16[2,896,128]{2,1,0:T(8,128)(2,1)S(1)} %shard_map.40.refs_0_), channel_id=1, source_target_pairs={{0,4},{1,13},{2,6},{3,15},{4,8},{5,1},{6,10},{7,3},{8,12},{9,5},{1... | collective-permute-start | bytes 1376264 | tf_op jit(solution)/shard_map/ppermute | solution.py:234
  66.0 23.5 %copy-start.3 = (bf16[16,32,128]{2,1,0:T(8,128)(2,1)}, bf16[16,32,128]{2,1,0:T(8,128)(2,1)S(1)}, u32[]{:S(2)}) copy-start(bf16[16,32,128]{2,1,0:T(8,128)(2,1)S(1)} %all_to_all.16.routed_ref) | copy-start | bytes 393220
  66.0 23.5 %copy-start.1 = (bf16[2,896,128]{2,1,0:T(8,128)(2,1)}, bf16[2,896,128]{2,1,0:T(8,128)(2,1)S(1)}, u32[]{:S(2)}) copy-start(bf16[2,896,128]{2,1,0:T(8,128)(2,1)S(1)} %collective-permute-done.1.after_ref.refs_2_) | copy-start | bytes 1376260
  67.1 27.1 %all-to-all-start.2 = ((bf16[8,16,24,128]{3,2,1,0:T(8,128)(2,1)}), bf16[8,16,24,128]{3,2,1,0:T(8,128)(2,1)S(1)}, u32[]{:S(2)}, u32[]{:S(2)}) async-start(bf16[8,16,24,128]{3,2,1,0:T(8,128)(2,1)} %shard_map.41), calls=%async_computation.2 | async-start | bytes 1572864 | tf_op jit(solution)/shard_map/all_to_all | solution.py:297
  70.7 12.5 %collective-permute-start.2 = (bf16[2,896,128]{2,1,0:T(8,128)(2,1)S(1)}, bf16[2,896,128]{2,1,0:T(8,128)(2,1)}, u32[]{:S(2)}, u32[]{:S(2)}) collective-permute-start(bf16[2,896,128]{2,1,0:T(8,128)(2,1)S(1)} %shard_map.40.refs_0_), channel_id=1, source_target_pairs={{0,2},{1,15},{2,4},{3,1},{4,6},{5,3},{6,8},{7,5},{8,10},{9,7},{10,... | collective-permute-start | bytes 1376264 | tf_op jit(solution)/shard_map/ppermute | solution.py:234
  73.8 12.5 %collective-permute-start.4 = (bf16[2,896,128]{2,1,0:T(8,128)(2,1)S(1)}, bf16[2,896,128]{2,1,0:T(8,128)(2,1)S(1)}, u32[]{:S(2)}, u32[]{:S(2)}) collective-permute-start(bf16[2,896,128]{2,1,0:T(8,128)(2,1)S(1)} %collective-permute-done.1.after_ref.refs_2_), channel_id=1, source_target_pairs={{0,2},{1,15},{2,4},{3,1},{4,6},{5,3},{6,8},{7,5},{8,10},{9,7},{10,... | collective-permute-start | bytes 1376264 | tf_op jit(solution)/shard_map/ppermute | solution.py:234
  79.3 10.2 %collective-permute-start.3 = (bf16[2,896,128]{2,1,0:T(8,128)(2,1)S(1)}, bf16[2,896,128]{2,1,0:T(8,128)(2,1)}, u32[]{:S(2)}, u32[]{:S(2)}) collective-permute-start(bf16[2,896,128]{2,1,0:T(8,128)(2,1)S(1)} %collective-permute-done.1.after_ref.refs_2_), channel_id=1, source_target_pairs={{0,1},{1,0},{2,3},{3,2},{4,5},{5,4},{6,7},{7,6},{8,9},{9,8},{10,11... | collective-permute-start | bytes 1376264 | tf_op jit(solution)/shard_map/ppermute | solution.py:238
  81.2 15.7 %collective-permute-start.7 = (bf16[2,896,128]{2,1,0:T(8,128)(2,1)S(1)}, bf16[2,896,128]{2,1,0:T(8,128)(2,1)S(1)}, u32[]{:S(2)}, u32[]{:S(2)}) collective-permute-start(bf16[2,896,128]{2,1,0:T(8,128)(2,1)S(1)} %collective-permute-done.1.after_ref.refs_2_), channel_id=1, source_target_pairs={{0,4},{1,13},{2,6},{3,15},{4,8},{5,1},{6,10},{7,3},{8,12},{9,5},{1... | collective-permute-start | bytes 1376264 | tf_op jit(solution)/shard_map/ppermute | solution.py:234
  83.2 13.6 %collective-permute-start.5 = (bf16[2,896,128]{2,1,0:T(8,128)(2,1)}, bf16[2,896,128]{2,1,0:T(8,128)(2,1)S(1)}, u32[]{:S(2)}, u32[]{:S(2)}) collective-permute-start(bf16[2,896,128]{2,1,0:T(8,128)(2,1)} %collective-permute-done.2.refs_1_), channel_id=1, source_target_pairs={{0,1},{1,0},{2,3},{3,2},{4,5},{5,4},{6,7},{7,6},{8,9},{9,8},{10,11... | collective-permute-start | bytes 1376264 | tf_op jit(solution)/shard_map/ppermute | solution.py:238
  86.3 3.2 %copy-start.7 = (bf16[2,896,128]{2,1,0:T(8,128)(2,1)}, bf16[2,896,128]{2,1,0:T(8,128)(2,1)S(1)}, u32[]{:S(2)}) copy-start(bf16[2,896,128]{2,1,0:T(8,128)(2,1)S(1)} %collective-permute-done.4.refs_4_) | copy-start | bytes 1376260
  86.3 10.5 %collective-permute-start.6 = (bf16[2,896,128]{2,1,0:T(8,128)(2,1)S(1)}, bf16[2,896,128]{2,1,0:T(8,128)(2,1)S(1)}, u32[]{:S(2)}, u32[]{:S(2)}) collective-permute-start(bf16[2,896,128]{2,1,0:T(8,128)(2,1)S(1)} %collective-permute-done.4.refs_4_), channel_id=1, source_target_pairs={{0,1},{1,0},{2,3},{3,2},{4,5},{5,4},{6,7},{7,6},{8,9},{9,8},{10,11... | collective-permute-start | bytes 1376264 | tf_op jit(solution)/shard_map/ppermute | solution.py:238
  94.2 1.8 %copy-start = (bf16[5248,256]{1,0:T(8,128)(2,1)S(1)}, bf16[5248,256]{1,0:T(8,128)(2,1)}, u32[]{:S(2)}) copy-start(bf16[5248,256]{1,0:T(8,128)(2,1)} %shard_map.43.early_ref) | copy-start | bytes 8060932

commit v5 on v4

--- a/solution.py
+++ b/solution.py
@@ -70,12 +70,18 @@
         ).astype(jnp.bfloat16)
 
 
-def copies_kernel(routed_ref, after_ref, slots_ref):
+def copies_kernel(routed_ref, after_ref, slots_ref, block_ref, sems):
     del after_ref
-    for g in range(OWNERS):
-        slots = routed_ref[g].astype(jnp.float32)[:HALF].astype(jnp.bfloat16)
-        for y in range(DB):
-            slots_ref[y, g] = slots
+    block_ref[...] = jnp.concatenate(
+        [routed_ref[g].astype(jnp.float32)[:HALF] for g in range(OWNERS)], axis=0
+    ).astype(jnp.bfloat16)
+    copies = [
+        pltpu.make_async_copy(block_ref, slots_ref.at[y], sems.at[y]) for y in range(DB)
+    ]
+    for copy in copies:
+        copy.start()
+    for copy in copies:
+        copy.wait()
 
 
 def send_kernel(tokens_ref, grads_ref, out_ref):
@@ -290,7 +296,12 @@
             pl.BlockSpec(memory_space=pltpu.VMEM),
             pl.BlockSpec(memory_space=pl.ANY),
         ],
-        out_shape=jax.ShapeDtypeStruct((DB, OWNERS, HALF, LANES), jnp.bfloat16),
+        out_specs=pl.BlockSpec(memory_space=pl.ANY),
+        out_shape=jax.ShapeDtypeStruct((DB, OWNERS * HALF, LANES), jnp.bfloat16),
+        scratch_shapes=[
+            pltpu.VMEM((OWNERS * HALF, LANES), jnp.bfloat16),
+            pltpu.SemaphoreType.DMA((DB,)),
+        ],
         cost_estimate=cost(1 << 20, 1 << 20),
         compiler_params=params(16),
     )(routed, next_)
@@ -312,7 +323,7 @@
         out_shape=jax.ShapeDtypeStruct((OWN, OWNERS, ROOM, FBLK), jnp.bfloat16),
         cost_estimate=cost(1 << 32, 2 << 20),
         compiler_params=params(12),
-    )(slots.reshape(DB, OWNERS * HALF, LANES))
+    )(slots)
     total = pl.pallas_call(
         first_kernel,
         in_specs=[scalar, vmem, vmem],

time: 99.7 us -> 102 us (1.023)
  Pallas kernels: 11.9 us -> 14.4 us
    pallas_call x1, Pallas kernels: 1.94 us -> 3.23 us  [body(): pl.pallas_call(last_kernel, in_specs=[scalar] + [vmem] * (3 + PAIRS - FIR...]
    pallas_call x1, Pallas kernels: 0.61 us -> 1.89 us  [body(): pl.pallas_call(value_kernel, out_shape=jax.ShapeDtypeStruct((OWN, OWNERS,...]
  transfers between devices with their start and end apart: 9 -> 9, of which waited for: 1 -> 0; matrix products, arithmetic and copies ran while one was open for 0% -> 0% of each run, Pallas kernels for 9% -> 10%
where the time goes in v5:
time: 102 us
  blocking collectives  50.6 us (50%)
  starting transfers between devices  33.5 us (33%)
  Pallas kernels  14.4 us (14%)
  local copies, waits for them, and re-layouts  2.76 us (3%)
    all_to_all x1, blocking collectives, body(): lax.all_to_all(send, ('y', 'z'), split_axis=0, concat_axis=0, tiled=True)  36.9 us
    ppermute x4, starting transfers between devices, ahead(): return lax.ppermute(value, OWNER, pairs)  15.9 us
    all_to_all x1, blocking collectives, body(): lax.all_to_all(routed, OWNER, split_axis=0, concat_axis=0, tiled=True)  13.7 us
    ppermute x4, starting transfers between devices, swap(): return lax.ppermute(value, 'core', [(0, 1), (1, 0)])  13.3 us
    pallas_call x1, Pallas kernels, body(): pl.pallas_call(early_kernel, in_specs=[scalar] + [vmem] * (1 + FIRST), ou...  4.35 us
    all_to_all x1, starting transfers between devices, body(): slots = lax.all_to_all(slots, 'y', split_axis=0, concat_axis=0, tiled=True)  4.23 us
    pallas_call x1, Pallas kernels, body(): pl.pallas_call(last_kernel, in_specs=[scalar] + [vmem] * (3 + PAIRS - FIR...  3.23 us
    unnamed x17, local copies, waits for them, and re-layouts  2.62 us
  transfers between devices with their start and end apart: 9, of which 0 were waited for; matrix products, arithmetic and copies ran while one was open for 0% of the time, Pallas kernels for 10%

profile of v5, /device:TPU:1, one launch (start us, length us, event | category | flops | bytes accessed | tf_op | source)
XLA Modules:
  0.0 101.5 jit_solution(5671752698018822001)
XLA Ops:
  0.0 0.8 copy-done.5
  0.8 0.7 copy-done.6
  1.6 0.2 shard_map.37
  1.8 36.9 %all_to_all.15 = bf16[64,2,1152]{2,1,0:T(2,128)(2,1)S(1)} all-to-all(bf16[64,2,1152]{2,1,0:T(2,128)(2,1)S(1)} %shard_map.37), channel_id=1, replica_groups=mesh['y'=8,'z'=8,'x'=8,'core'=2] {'y','z'}, dimensions={0} | all-to-all | bytes 589824 | tf_op jit(solution)/shard_map/all_to_all | solution.py:262
  38.8 0.1 reshape.7
  38.9 0.2 copy.9
  39.1 5.0 %collective-permute-start = (bf16[896,128]{1,0:T(8,128)(2,1)S(1)}, bf16[896,128]{1,0:T(8,128)(2,1)S(1)}, u32[]{:S(2)}, u32[]{:S(2)}) collective-permute-start(bf16[896,128]{1,0:T(8,128)(2,1)S(1)} %bitcast.10), channel_id=1, source_target_pairs={{0,1},{1,0},{2,3},{3,2},{4,5},{5,4},{6,7},{7,6},{8,9},{9,8},{10,11... | collective-permute-start | bytes 688136 | tf_op jit(solution)/shard_map/ppermute | solution.py:244
  44.2 1.7 %shard_map.38.onehot_ref.after_ref = bf16[384,4096]{1,0:T(8,128)(2,1)S(1)} custom-call(s32[8,128]{1,0:T(8,128)S(1)} %bitcast.12), custom_call_target="tpu_custom_call" | custom-call | flops 4194304 | bytes 6291456 | tf_op jit(solution)/shard_map/pallas_call | solution.py:249
  45.9 0.0 collective-permute-done.other_ref
  45.9 5.4 %collective-permute-start.1 = (bf16[2,896,128]{2,1,0:T(8,128)(2,1)S(1)}, bf16[2,896,128]{2,1,0:T(8,128)(2,1)S(1)}, u32[]{:S(2)}, u32[]{:S(2)}) collective-permute-start(bf16[2,896,128]{2,1,0:T(8,128)(2,1)S(1)} %shard_map.40.refs_0_), channel_id=1, source_target_pairs={{0,4},{1,13},{2,6},{3,15},{4,8},{5,1},{6,10},{7,3},{8,12},{9,5},{1... | collective-permute-start | bytes 1376264 | tf_op jit(solution)/shard_map/ppermute | solution.py:240
  51.3 1.0 %shard_map.39 = bf16[16,32,128]{2,1,0:T(8,128)(2,1)S(1)} custom-call(bf16[128,256]{1,0:T(8,128)(2,1)S(1)} %slice.9.pieces_ref, bf16[384,4096]{1,0:T(8,128)(2,1)S(1)} %shard_map.38.onehot_ref.after_ref, s32[8,128]{1,0:T(8,128)S(1)} %bitcast.13), custom_call_target="tpu_custom_call" | custom-call | flops 536870912 | bytes 4194304 | tf_op jit(solution)/shard_map/pallas_call | solution.py:285
  52.3 13.7 %all_to_all.16.routed_ref = bf16[16,32,128]{2,1,0:T(8,128)(2,1)S(1)} all-to-all(bf16[16,32,128]{2,1,0:T(8,128)(2,1)S(1)} %shard_map.39), channel_id=1, replica_groups=mesh['y'=8,'z'=8,'x'=8,'core'=2] {'x','core'}, dimensions={0} | all-to-all | bytes 262144 | tf_op jit(solution)/shard_map/all_to_all | solution.py:292
  66.0 0.0 collective-permute-done.1.after_ref.refs_2_
  66.1 1.1 %shard_map.41 = bf16[8,384,128]{2,1,0:T(8,128)(2,1)} custom-call(bf16[16,32,128]{2,1,0:T(8,128)(2,1)S(1)} %all_to_all.16.routed_ref, bf16[2,896,128]{2,1,0:T(8,128)(2,1)S(1)} %collective-permute-done.1.after_ref.refs_2_), custom_call_target="tpu_custom_call" | custom-call | flops 1048576 | bytes 1048576 | tf_op jit(solution)/shard_map/pallas_call | solution.py:293
  67.1 4.2 %all-to-all-start.2 = ((bf16[8,384,128]{2,1,0:T(8,128)(2,1)}), bf16[8,384,128]{2,1,0:T(8,128)(2,1)}, u32[]{:S(2)}, u32[]{:S(2)}) async-start(bf16[8,384,128]{2,1,0:T(8,128)(2,1)} %shard_map.41), calls=%async_computation.2 | async-start | bytes 1572864 | tf_op jit(solution)/shard_map/all_to_all | solution.py:308
  71.4 3.1 %collective-permute-start.2 = (bf16[2,896,128]{2,1,0:T(8,128)(2,1)S(1)}, bf16[2,896,128]{2,1,0:T(8,128)(2,1)}, u32[]{:S(2)}, u32[]{:S(2)}) collective-permute-start(bf16[2,896,128]{2,1,0:T(8,128)(2,1)S(1)} %shard_map.40.refs_0_), channel_id=1, source_target_pairs={{0,2},{1,15},{2,4},{3,1},{4,6},{5,3},{6,8},{7,5},{8,10},{9,7},{10,... | collective-permute-start | bytes 1376264 | tf_op jit(solution)/shard_map/ppermute | solution.py:240
  74.5 5.4 %collective-permute-start.4 = (bf16[2,896,128]{2,1,0:T(8,128)(2,1)S(1)}, bf16[2,896,128]{2,1,0:T(8,128)(2,1)}, u32[]{:S(2)}, u32[]{:S(2)}) collective-permute-start(bf16[2,896,128]{2,1,0:T(8,128)(2,1)S(1)} %collective-permute-done.1.after_ref.refs_2_), channel_id=1, source_target_pairs={{0,2},{1,15},{2,4},{3,1},{4,6},{5,3},{6,8},{7,5},{8,10},{9,7},{10,... | collective-permute-start | bytes 1376264 | tf_op jit(solution)/shard_map/ppermute | solution.py:240
  79.9 1.9 %collective-permute-start.3 = (bf16[2,896,128]{2,1,0:T(8,128)(2,1)S(1)}, bf16[2,896,128]{2,1,0:T(8,128)(2,1)S(1)}, u32[]{:S(2)}, u32[]{:S(2)}) collective-permute-start(bf16[2,896,128]{2,1,0:T(8,128)(2,1)S(1)} %collective-permute-done.1.after_ref.refs_2_), channel_id=1, source_target_pairs={{0,1},{1,0},{2,3},{3,2},{4,5},{5,4},{6,7},{7,6},{8,9},{9,8},{10,11... | collective-permute-start | bytes 1376264 | tf_op jit(solution)/shard_map/ppermute | solution.py:244
  81.9 2.0 %collective-permute-start.7 = (bf16[2,896,128]{2,1,0:T(8,128)(2,1)S(1)}, bf16[2,896,128]{2,1,0:T(8,128)(2,1)}, u32[]{:S(2)}, u32[]{:S(2)}) collective-permute-start(bf16[2,896,128]{2,1,0:T(8,128)(2,1)S(1)} %collective-permute-done.1.after_ref.refs_2_), channel_id=1, source_target_pairs={{0,4},{1,13},{2,6},{3,15},{4,8},{5,1},{6,10},{7,3},{8,12},{9,5},{1... | collective-permute-start | bytes 1376264 | tf_op jit(solution)/shard_map/ppermute | solution.py:240
  83.9 0.0 collective-permute-done.2.refs_1_
  83.9 3.1 %collective-permute-start.5 = (bf16[2,896,128]{2,1,0:T(8,128)(2,1)}, bf16[2,896,128]{2,1,0:T(8,128)(2,1)}, u32[]{:S(2)}, u32[]{:S(2)}) collective-permute-start(bf16[2,896,128]{2,1,0:T(8,128)(2,1)} %collective-permute-done.2.refs_1_), channel_id=1, source_target_pairs={{0,1},{1,0},{2,3},{3,2},{4,5},{5,4},{6,7},{7,6},{8,9},{9,8},{10,11... | collective-permute-start | bytes 1376264 | tf_op jit(solution)/shard_map/ppermute | solution.py:244
  87.0 0.0 collective-permute-done.4.refs_4_
  87.0 3.2 %collective-permute-start.6 = (bf16[2,896,128]{2,1,0:T(8,128)(2,1)}, bf16[2,896,128]{2,1,0:T(8,128)(2,1)}, u32[]{:S(2)}, u32[]{:S(2)}) collective-permute-start(bf16[2,896,128]{2,1,0:T(8,128)(2,1)} %collective-permute-done.4.refs_4_), channel_id=1, source_target_pairs={{0,1},{1,0},{2,3},{3,2},{4,5},{5,4},{6,7},{7,6},{8,9},{9,8},{10,11... | collective-permute-start | bytes 1376264 | tf_op jit(solution)/shard_map/ppermute | solution.py:244
  90.3 0.0 collective-permute-done.3.refs_3_
  90.3 0.8 copy-done.7
  91.1 4.3 %shard_map.43.early_ref = bf16[5248,256]{1,0:T(8,128)(2,1)} custom-call(s32[1]{0:T(128)} %bitcast.me_ref, bf16[16,32,128]{2,1,0:T(8,128)(2,1)} %copy-done.3, bf16[2,896,128]{2,1,0:T(8,128)(2,1)} %copy-done.2, bf16[2,896,128]{2,1,0:T(8,128)(2,1)} %collective-permute-done.2.refs_1_, bf16[2,896,128]{2,1,0:T(8,128)(2,1)} %copy-done.1, ...), custom_call_target="tpu_custom_call" | custom-call | flops 1073741824 | bytes 4194304 | tf_op jit(solution)/shard_map/pallas_call | solution.py:312
  95.4 1.9 %shard_map.42.value_ref = bf16[2,16,64,256]{3,2,1,0:T(8,128)(2,1)S(1)} custom-call(bf16[8,384,128]{2,1,0:T(8,128)(2,1)} %all-to-all-done.2.slots_ref), custom_call_target="tpu_custom_call" | custom-call | flops 4294967296 | bytes 2097152 | tf_op jit(solution)/shard_map/pallas_call | solution.py:321
  97.3 0.1 copy-done
  97.4 0.9 shard_map.44.total_ref
  98.3 0.0 collective-permute-done.7.refs_2_
  98.3 0.0 collective-permute-done.6.refs_1_
  98.3 3.2 %shard_map.45 = bf16[2,896,256]{2,1,0:T(8,128)(2,1)} custom-call(s32[1]{0:T(128)} %bitcast.me_ref, bf16[2,16,64,256]{3,2,1,0:T(8,128)(2,1)S(1)} %shard_map.42.value_ref, bf16[5248,256]{1,0:T(8,128)(2,1)S(1)} %copy-done, f32[2,896,256]{2,1,0:T(8,128)S(1)} %shard_map.44.total_ref, bf16[2,896,128]{2,1,0:T(8,128)(2,1)} %collective-permute-done.5.refs_0_, ...), custom_call_target="tpu_custom_call" | custom-call | flops 1073741824 | bytes 5242880 | tf_op jit(solution)/shard_map/pallas_call | solution.py:335
  (17 shorter events, 0.1 us)
Async XLA Ops:
  0.0 0.8 copy-start.5
  0.8 0.7 copy-start.6
  1.6 42.6 %copy-start.4 = (s32[1,128,8]{1,2,0:T(8,128)S(1)}, s32[1,128,8]{1,2,0:T(8,128)}, u32[]{:S(2)}) copy-start(s32[1,128,8]{1,2,0:T(8,128)} %param.5) | copy-start | bytes 12292
  39.1 6.8 %collective-permute-start = (bf16[896,128]{1,0:T(8,128)(2,1)S(1)}, bf16[896,128]{1,0:T(8,128)(2,1)S(1)}, u32[]{:S(2)}, u32[]{:S(2)}) collective-permute-start(bf16[896,128]{1,0:T(8,128)(2,1)S(1)} %bitcast.10), channel_id=1, source_target_pairs={{0,1},{1,0},{2,3},{3,2},{4,5},{5,4},{6,7},{7,6},{8,9},{9,8},{10,11... | collective-permute-start | bytes 688136 | tf_op jit(solution)/shard_map/ppermute | solution.py:244
  45.9 25.5 %copy-start.2 = (bf16[2,896,128]{2,1,0:T(8,128)(2,1)}, bf16[2,896,128]{2,1,0:T(8,128)(2,1)S(1)}, u32[]{:S(2)}) copy-start(bf16[2,896,128]{2,1,0:T(8,128)(2,1)S(1)} %shard_map.40.refs_0_) | copy-start | bytes 1376260
  45.9 20.1 %collective-permute-start.1 = (bf16[2,896,128]{2,1,0:T(8,128)(2,1)S(1)}, bf16[2,896,128]{2,1,0:T(8,128)(2,1)S(1)}, u32[]{:S(2)}, u32[]{:S(2)}) collective-permute-start(bf16[2,896,128]{2,1,0:T(8,128)(2,1)S(1)} %shard_map.40.refs_0_), channel_id=1, source_target_pairs={{0,4},{1,13},{2,6},{3,15},{4,8},{5,1},{6,10},{7,3},{8,12},{9,5},{1... | collective-permute-start | bytes 1376264 | tf_op jit(solution)/shard_map/ppermute | solution.py:240
  66.0 24.3 %copy-start.3 = (bf16[16,32,128]{2,1,0:T(8,128)(2,1)}, bf16[16,32,128]{2,1,0:T(8,128)(2,1)S(1)}, u32[]{:S(2)}) copy-start(bf16[16,32,128]{2,1,0:T(8,128)(2,1)S(1)} %all_to_all.16.routed_ref) | copy-start | bytes 393220
  66.0 24.3 %copy-start.1 = (bf16[2,896,128]{2,1,0:T(8,128)(2,1)}, bf16[2,896,128]{2,1,0:T(8,128)(2,1)S(1)}, u32[]{:S(2)}) copy-start(bf16[2,896,128]{2,1,0:T(8,128)(2,1)S(1)} %collective-permute-done.1.after_ref.refs_2_) | copy-start | bytes 1376260
  67.1 28.3 %all-to-all-start.2 = ((bf16[8,384,128]{2,1,0:T(8,128)(2,1)}), bf16[8,384,128]{2,1,0:T(8,128)(2,1)}, u32[]{:S(2)}, u32[]{:S(2)}) async-start(bf16[8,384,128]{2,1,0:T(8,128)(2,1)} %shard_map.41), calls=%async_computation.2 | async-start | bytes 1572864 | tf_op jit(solution)/shard_map/all_to_all | solution.py:308
  71.4 12.5 %collective-permute-start.2 = (bf16[2,896,128]{2,1,0:T(8,128)(2,1)S(1)}, bf16[2,896,128]{2,1,0:T(8,128)(2,1)}, u32[]{:S(2)}, u32[]{:S(2)}) collective-permute-start(bf16[2,896,128]{2,1,0:T(8,128)(2,1)S(1)} %shard_map.40.refs_0_), channel_id=1, source_target_pairs={{0,2},{1,15},{2,4},{3,1},{4,6},{5,3},{6,8},{7,5},{8,10},{9,7},{10,... | collective-permute-start | bytes 1376264 | tf_op jit(solution)/shard_map/ppermute | solution.py:240
  74.5 12.5 %collective-permute-start.4 = (bf16[2,896,128]{2,1,0:T(8,128)(2,1)S(1)}, bf16[2,896,128]{2,1,0:T(8,128)(2,1)}, u32[]{:S(2)}, u32[]{:S(2)}) collective-permute-start(bf16[2,896,128]{2,1,0:T(8,128)(2,1)S(1)} %collective-permute-done.1.after_ref.refs_2_), channel_id=1, source_target_pairs={{0,2},{1,15},{2,4},{3,1},{4,6},{5,3},{6,8},{7,5},{8,10},{9,7},{10,... | collective-permute-start | bytes 1376264 | tf_op jit(solution)/shard_map/ppermute | solution.py:240
  79.9 10.3 %collective-permute-start.3 = (bf16[2,896,128]{2,1,0:T(8,128)(2,1)S(1)}, bf16[2,896,128]{2,1,0:T(8,128)(2,1)S(1)}, u32[]{:S(2)}, u32[]{:S(2)}) collective-permute-start(bf16[2,896,128]{2,1,0:T(8,128)(2,1)S(1)} %collective-permute-done.1.after_ref.refs_2_), channel_id=1, source_target_pairs={{0,1},{1,0},{2,3},{3,2},{4,5},{5,4},{6,7},{7,6},{8,9},{9,8},{10,11... | collective-permute-start | bytes 1376264 | tf_op jit(solution)/shard_map/ppermute | solution.py:244
  81.9 16.4 %collective-permute-start.7 = (bf16[2,896,128]{2,1,0:T(8,128)(2,1)S(1)}, bf16[2,896,128]{2,1,0:T(8,128)(2,1)}, u32[]{:S(2)}, u32[]{:S(2)}) collective-permute-start(bf16[2,896,128]{2,1,0:T(8,128)(2,1)S(1)} %collective-permute-done.1.after_ref.refs_2_), channel_id=1, source_target_pairs={{0,4},{1,13},{2,6},{3,15},{4,8},{5,1},{6,10},{7,3},{8,12},{9,5},{1... | collective-permute-start | bytes 1376264 | tf_op jit(solution)/shard_map/ppermute | solution.py:240
  83.9 14.4 %collective-permute-start.5 = (bf16[2,896,128]{2,1,0:T(8,128)(2,1)}, bf16[2,896,128]{2,1,0:T(8,128)(2,1)}, u32[]{:S(2)}, u32[]{:S(2)}) collective-permute-start(bf16[2,896,128]{2,1,0:T(8,128)(2,1)} %collective-permute-done.2.refs_1_), channel_id=1, source_target_pairs={{0,1},{1,0},{2,3},{3,2},{4,5},{5,4},{6,7},{7,6},{8,9},{9,8},{10,11... | collective-permute-start | bytes 1376264 | tf_op jit(solution)/shard_map/ppermute | solution.py:244
  87.0 11.3 %collective-permute-start.6 = (bf16[2,896,128]{2,1,0:T(8,128)(2,1)}, bf16[2,896,128]{2,1,0:T(8,128)(2,1)}, u32[]{:S(2)}, u32[]{:S(2)}) collective-permute-start(bf16[2,896,128]{2,1,0:T(8,128)(2,1)} %collective-permute-done.4.refs_4_), channel_id=1, source_target_pairs={{0,1},{1,0},{2,3},{3,2},{4,5},{5,4},{6,7},{7,6},{8,9},{9,8},{10,11... | collective-permute-start | bytes 1376264 | tf_op jit(solution)/shard_map/ppermute | solution.py:244
  90.3 0.8 copy-start.7
  95.4 2.0 %copy-start = (bf16[5248,256]{1,0:T(8,128)(2,1)S(1)}, bf16[5248,256]{1,0:T(8,128)(2,1)}, u32[]{:S(2)}) copy-start(bf16[5248,256]{1,0:T(8,128)(2,1)} %shard_map.43.early_ref) | copy-start | bytes 8060932

commit v6 on v4

--- a/solution.py
+++ b/solution.py
@@ -18,7 +18,7 @@
 OWNERS = 16
 HALF = CAP // 2
 LANES = 128
-FIRST = 5
+FIRST = 4
 PAIRS = 8
 ROOM = 64
 XS = 8
@@ -115,8 +115,8 @@
         (0, core),
         (-1, core),
         (-2, core),
+        (-3, core),
         (2, 1 - core),
-        (-3, core),
         (1, 1 - core),
         (3, 1 - core),
         (4, core),
@@ -306,7 +306,7 @@
         ),
         cost_estimate=cost(1 << 30, 4 << 20),
         compiler_params=params(60),
-    )(me, routed, here, near, next_, swap(next_), third)
+    )(me, routed, here, near, next_, third)
     value = pl.pallas_call(
         value_kernel,
         out_shape=jax.ShapeDtypeStruct((OWN, OWNERS, ROOM, FBLK), jnp.bfloat16),
@@ -327,7 +327,7 @@
         out_shape=jax.ShapeDtypeStruct((OWN, DBLK, FBLK), jnp.bfloat16),
         cost_estimate=cost(1 << 30, 5 << 20),
         compiler_params=params(16),
-    )(me, value, early, total, swap(near), swap(third), far)
+    )(me, value, early, total, swap(next_), swap(near), swap(third), far)
     return out[:, None]
 
 

time: 99.7 us -> 99.5 us (level)
    unnamed x17 -> x15, local copies, waits for them, and re-layouts: 2.92 us -> 2.82 us
  transfers between devices with their start and end apart: 9 -> 9, of which waited for: 1 -> 2; matrix products, arithmetic and copies ran while one was open for 0% -> 0% of each run, Pallas kernels for 9% -> 8%
where the time goes in v6:
time: 99.5 us; the launch traced here: 98.8 us
  blocking collectives  50.6 us (51%)
  starting transfers between devices  32.8 us (33%)
  Pallas kernels  11.4 us (11%)
  local copies, waits for them, and re-layouts  2.96 us (3%)
    all_to_all x1, blocking collectives, body(): lax.all_to_all(send, ('y', 'z'), split_axis=0, concat_axis=0, tiled=True)  36.9 us
    ppermute x4, starting transfers between devices, ahead(): return lax.ppermute(value, OWNER, pairs)  15.9 us
    all_to_all x1, blocking collectives, body(): lax.all_to_all(routed, OWNER, split_axis=0, concat_axis=0, tiled=True)  13.7 us
    ppermute x4, starting transfers between devices, swap(): return lax.ppermute(value, 'core', [(0, 1), (1, 0)])  13.3 us
    pallas_call x1, Pallas kernels, body(): pl.pallas_call(early_kernel, in_specs=[scalar] + [vmem] * (1 + FIRST), ou...  4.04 us
    all_to_all x1, starting transfers between devices, body(): slots = lax.all_to_all(slots, 'y', split_axis=0, concat_axis=0, tiled=True)  3.55 us
    unnamed x15, local copies, waits for them, and re-layouts  2.82 us
    pallas_call x1, Pallas kernels, body(): pl.pallas_call(last_kernel, in_specs=[scalar] + [vmem] * (3 + PAIRS - FIR...  2.08 us
  transfers between devices with their start and end apart: 9, of which 2 were waited for; matrix products, arithmetic and copies ran while one was open for 0% of the time, Pallas kernels for 8%

profile of v6, /device:TPU:1, one launch (start us, length us, event | category | flops | bytes accessed | tf_op | source)
XLA Modules:
  0.0 98.8 jit_solution(4368755966020971008)
XLA Ops:
  0.0 0.8 copy-done.5
  0.8 0.7 copy-done.6
  1.6 0.2 shard_map.37
  1.8 36.9 %all_to_all.15 = bf16[64,2,1152]{2,1,0:T(2,128)(2,1)S(1)} all-to-all(bf16[64,2,1152]{2,1,0:T(2,128)(2,1)S(1)} %shard_map.37), channel_id=1, replica_groups=mesh['y'=8,'z'=8,'x'=8,'core'=2] {'y','z'}, dimensions={0} | all-to-all | bytes 589824 | tf_op jit(solution)/shard_map/all_to_all | solution.py:256
  38.8 0.1 reshape.10
  38.9 0.2 copy.9
  39.1 5.0 %collective-permute-start = (bf16[896,128]{1,0:T(8,128)(2,1)S(1)}, bf16[896,128]{1,0:T(8,128)(2,1)S(1)}, u32[]{:S(2)}, u32[]{:S(2)}) collective-permute-start(bf16[896,128]{1,0:T(8,128)(2,1)S(1)} %bitcast.11), channel_id=1, source_target_pairs={{0,1},{1,0},{2,3},{3,2},{4,5},{5,4},{6,7},{7,6},{8,9},{9,8},{10,11... | collective-permute-start | bytes 688136 | tf_op jit(solution)/shard_map/ppermute | solution.py:238
  44.1 1.7 %shard_map.38.onehot_ref.after_ref = bf16[384,4096]{1,0:T(8,128)(2,1)S(1)} custom-call(s32[8,128]{1,0:T(8,128)S(1)} %bitcast.14), custom_call_target="tpu_custom_call" | custom-call | flops 4194304 | bytes 6291456 | tf_op jit(solution)/shard_map/pallas_call | solution.py:243
  45.8 0.0 collective-permute-done.other_ref
  45.9 5.4 %collective-permute-start.1 = (bf16[2,896,128]{2,1,0:T(8,128)(2,1)S(1)}, bf16[2,896,128]{2,1,0:T(8,128)(2,1)S(1)}, u32[]{:S(2)}, u32[]{:S(2)}) collective-permute-start(bf16[2,896,128]{2,1,0:T(8,128)(2,1)S(1)} %shard_map.40.refs_0_), channel_id=1, source_target_pairs={{0,4},{1,13},{2,6},{3,15},{4,8},{5,1},{6,10},{7,3},{8,12},{9,5},{1... | collective-permute-start | bytes 1376264 | tf_op jit(solution)/shard_map/ppermute | solution.py:234
  51.3 1.0 %shard_map.39 = bf16[16,32,128]{2,1,0:T(8,128)(2,1)S(1)} custom-call(bf16[128,256]{1,0:T(8,128)(2,1)S(1)} %slice.9.pieces_ref, bf16[384,4096]{1,0:T(8,128)(2,1)S(1)} %shard_map.38.onehot_ref.after_ref, s32[8,128]{1,0:T(8,128)S(1)} %bitcast.15), custom_call_target="tpu_custom_call" | custom-call | flops 536870912 | bytes 4194304 | tf_op jit(solution)/shard_map/pallas_call | solution.py:279
  52.3 13.7 %all_to_all.16.routed_ref = bf16[16,32,128]{2,1,0:T(8,128)(2,1)S(1)} all-to-all(bf16[16,32,128]{2,1,0:T(8,128)(2,1)S(1)} %shard_map.39), channel_id=1, replica_groups=mesh['y'=8,'z'=8,'x'=8,'core'=2] {'x','core'}, dimensions={0} | all-to-all | bytes 262144 | tf_op jit(solution)/shard_map/all_to_all | solution.py:286
  66.0 1.1 %shard_map.41 = bf16[8,16,24,128]{3,2,1,0:T(8,128)(2,1)} custom-call(bf16[16,32,128]{2,1,0:T(8,128)(2,1)S(1)} %all_to_all.16.routed_ref, bf16[2,896,128]{2,1,0:T(8,128)(2,1)S(1)} %collective-permute-done.1.after_ref.refs_2_), custom_call_target="tpu_custom_call" | custom-call | flops 1048576 | bytes 1048576 | tf_op jit(solution)/shard_map/pallas_call | solution.py:287
  67.1 3.5 %all-to-all-start.2 = ((bf16[8,16,24,128]{3,2,1,0:T(8,128)(2,1)}), bf16[8,16,24,128]{3,2,1,0:T(8,128)(2,1)S(1)}, u32[]{:S(2)}, u32[]{:S(2)}) async-start(bf16[8,16,24,128]{3,2,1,0:T(8,128)(2,1)} %shard_map.41), calls=%async_computation.2 | async-start | bytes 1572864 | tf_op jit(solution)/shard_map/all_to_all | solution.py:297
  70.7 3.1 %collective-permute-start.2 = (bf16[2,896,128]{2,1,0:T(8,128)(2,1)S(1)}, bf16[2,896,128]{2,1,0:T(8,128)(2,1)}, u32[]{:S(2)}, u32[]{:S(2)}) collective-permute-start(bf16[2,896,128]{2,1,0:T(8,128)(2,1)S(1)} %shard_map.40.refs_0_), channel_id=1, source_target_pairs={{0,2},{1,15},{2,4},{3,1},{4,6},{5,3},{6,8},{7,5},{8,10},{9,7},{10,... | collective-permute-start | bytes 1376264 | tf_op jit(solution)/shard_map/ppermute | solution.py:234
  73.8 5.4 %collective-permute-start.3 = (bf16[2,896,128]{2,1,0:T(8,128)(2,1)S(1)}, bf16[2,896,128]{2,1,0:T(8,128)(2,1)}, u32[]{:S(2)}, u32[]{:S(2)}) collective-permute-start(bf16[2,896,128]{2,1,0:T(8,128)(2,1)S(1)} %collective-permute-done.1.after_ref.refs_2_), channel_id=1, source_target_pairs={{0,2},{1,15},{2,4},{3,1},{4,6},{5,3},{6,8},{7,5},{8,10},{9,7},{10,... | collective-permute-start | bytes 1376264 | tf_op jit(solution)/shard_map/ppermute | solution.py:234
  79.3 2.0 %collective-permute-start.7 = (bf16[2,896,128]{2,1,0:T(8,128)(2,1)S(1)}, bf16[2,896,128]{2,1,0:T(8,128)(2,1)S(1)}, u32[]{:S(2)}, u32[]{:S(2)}) collective-permute-start(bf16[2,896,128]{2,1,0:T(8,128)(2,1)S(1)} %collective-permute-done.1.after_ref.refs_2_), channel_id=1, source_target_pairs={{0,4},{1,13},{2,6},{3,15},{4,8},{5,1},{6,10},{7,3},{8,12},{9,5},{1... | collective-permute-start | bytes 1376264 | tf_op jit(solution)/shard_map/ppermute | solution.py:234
  81.3 3.1 %collective-permute-start.4 = (bf16[2,896,128]{2,1,0:T(8,128)(2,1)S(1)}, bf16[2,896,128]{2,1,0:T(8,128)(2,1)S(1)}, u32[]{:S(2)}, u32[]{:S(2)}) collective-permute-start(bf16[2,896,128]{2,1,0:T(8,128)(2,1)S(1)} %collective-permute-done.1.after_ref.refs_2_), channel_id=1, source_target_pairs={{0,1},{1,0},{2,3},{3,2},{4,5},{5,4},{6,7},{7,6},{8,9},{9,8},{10,11... | collective-permute-start | bytes 1376264 | tf_op jit(solution)/shard_map/ppermute | solution.py:238
  84.4 0.0 collective-permute-done.2.refs_1_
  84.4 1.9 %collective-permute-start.5 = (bf16[2,896,128]{2,1,0:T(8,128)(2,1)}, bf16[2,896,128]{2,1,0:T(8,128)(2,1)S(1)}, u32[]{:S(2)}, u32[]{:S(2)}) collective-permute-start(bf16[2,896,128]{2,1,0:T(8,128)(2,1)} %collective-permute-done.2.refs_1_), channel_id=1, source_target_pairs={{0,1},{1,0},{2,3},{3,2},{4,5},{5,4},{6,7},{7,6},{8,9},{9,8},{10,11... | collective-permute-start | bytes 1376264 | tf_op jit(solution)/shard_map/ppermute | solution.py:238
  86.3 0.0 collective-permute-done.3.refs_3_
  86.3 3.2 %collective-permute-start.6 = (bf16[2,896,128]{2,1,0:T(8,128)(2,1)}, bf16[2,896,128]{2,1,0:T(8,128)(2,1)S(1)}, u32[]{:S(2)}, u32[]{:S(2)}) collective-permute-start(bf16[2,896,128]{2,1,0:T(8,128)(2,1)} %collective-permute-done.3.refs_3_), channel_id=1, source_target_pairs={{0,1},{1,0},{2,3},{3,2},{4,5},{5,4},{6,7},{7,6},{8,9},{9,8},{10,11... | collective-permute-start | bytes 1376264 | tf_op jit(solution)/shard_map/ppermute | solution.py:238
  89.6 4.0 %shard_map.43.early_ref = bf16[4608,256]{1,0:T(8,128)(2,1)} custom-call(s32[1]{0:T(128)} %bitcast.me_ref, bf16[16,32,128]{2,1,0:T(8,128)(2,1)} %copy-done.3, bf16[2,896,128]{2,1,0:T(8,128)(2,1)} %copy-done.2, bf16[2,896,128]{2,1,0:T(8,128)(2,1)} %collective-permute-done.2.refs_1_, bf16[2,896,128]{2,1,0:T(8,128)(2,1)} %copy-done.1, ...), custom_call_target="tpu_custom_call" | custom-call | flops 1073741824 | bytes 4194304 | tf_op jit(solution)/shard_map/pallas_call | solution.py:301
  93.6 0.6 all-to-all-done.2
  94.2 0.6 shard_map.42.value_ref
  94.8 1.0 %copy-done = bf16[4608,256]{1,0:T(8,128)(2,1)S(1)} copy-done((bf16[4608,256]{1,0:T(8,128)(2,1)S(1)}, bf16[4608,256]{1,0:T(8,128)(2,1)}, u32[]{:S(2)}) %copy-start) | copy-done | bytes 2359320
  95.9 0.6 shard_map.44.total_ref
  96.5 0.0 collective-permute-done.5.refs_1_
  96.5 0.2 collective-permute-done.7.refs_3_
  96.7 0.0 collective-permute-done.4.refs_0_
  96.7 0.0 collective-permute-done.6.refs_2_
  96.7 2.1 %shard_map.45 = bf16[2,896,256]{2,1,0:T(8,128)(2,1)} custom-call(s32[1]{0:T(128)} %bitcast.me_ref, bf16[2,16,64,256]{3,2,1,0:T(8,128)(2,1)S(1)} %shard_map.42.value_ref, bf16[4608,256]{1,0:T(8,128)(2,1)S(1)} %copy-done, f32[2,896,256]{2,1,0:T(8,128)S(1)} %shard_map.44.total_ref, bf16[2,896,128]{2,1,0:T(8,128)(2,1)S(1)} %collective-permute-done.4.refs_0_, ...), custom_call_target="tpu_custom_call" | custom-call | flops 1073741824 | bytes 5242880 | tf_op jit(solution)/shard_map/pallas_call | solution.py:324
  (15 shorter events, 0.1 us)
Async XLA Ops:
  0.0 0.8 copy-start.5
  0.8 0.7 copy-start.6
  1.6 42.6 %copy-start.4 = (s32[1,128,8]{1,2,0:T(8,128)S(1)}, s32[1,128,8]{1,2,0:T(8,128)}, u32[]{:S(2)}) copy-start(s32[1,128,8]{1,2,0:T(8,128)} %param.5) | copy-start | bytes 12292
  39.1 6.8 %collective-permute-start = (bf16[896,128]{1,0:T(8,128)(2,1)S(1)}, bf16[896,128]{1,0:T(8,128)(2,1)S(1)}, u32[]{:S(2)}, u32[]{:S(2)}) collective-permute-start(bf16[896,128]{1,0:T(8,128)(2,1)S(1)} %bitcast.11), channel_id=1, source_target_pairs={{0,1},{1,0},{2,3},{3,2},{4,5},{5,4},{6,7},{7,6},{8,9},{9,8},{10,11... | collective-permute-start | bytes 688136 | tf_op jit(solution)/shard_map/ppermute | solution.py:238
  45.9 24.8 %copy-start.2 = (bf16[2,896,128]{2,1,0:T(8,128)(2,1)}, bf16[2,896,128]{2,1,0:T(8,128)(2,1)S(1)}, u32[]{:S(2)}) copy-start(bf16[2,896,128]{2,1,0:T(8,128)(2,1)S(1)} %shard_map.40.refs_0_) | copy-start | bytes 1376260
  45.9 20.1 %collective-permute-start.1 = (bf16[2,896,128]{2,1,0:T(8,128)(2,1)S(1)}, bf16[2,896,128]{2,1,0:T(8,128)(2,1)S(1)}, u32[]{:S(2)}, u32[]{:S(2)}) collective-permute-start(bf16[2,896,128]{2,1,0:T(8,128)(2,1)S(1)} %shard_map.40.refs_0_), channel_id=1, source_target_pairs={{0,4},{1,13},{2,6},{3,15},{4,8},{5,1},{6,10},{7,3},{8,12},{9,5},{1... | collective-permute-start | bytes 1376264 | tf_op jit(solution)/shard_map/ppermute | solution.py:234
  66.0 23.5 %copy-start.3 = (bf16[16,32,128]{2,1,0:T(8,128)(2,1)}, bf16[16,32,128]{2,1,0:T(8,128)(2,1)S(1)}, u32[]{:S(2)}) copy-start(bf16[16,32,128]{2,1,0:T(8,128)(2,1)S(1)} %all_to_all.16.routed_ref) | copy-start | bytes 393220
  66.0 23.5 %copy-start.1 = (bf16[2,896,128]{2,1,0:T(8,128)(2,1)}, bf16[2,896,128]{2,1,0:T(8,128)(2,1)S(1)}, u32[]{:S(2)}) copy-start(bf16[2,896,128]{2,1,0:T(8,128)(2,1)S(1)} %collective-permute-done.1.after_ref.refs_2_) | copy-start | bytes 1376260
  67.1 27.1 %all-to-all-start.2 = ((bf16[8,16,24,128]{3,2,1,0:T(8,128)(2,1)}), bf16[8,16,24,128]{3,2,1,0:T(8,128)(2,1)S(1)}, u32[]{:S(2)}, u32[]{:S(2)}) async-start(bf16[8,16,24,128]{3,2,1,0:T(8,128)(2,1)} %shard_map.41), calls=%async_computation.2 | async-start | bytes 1572864 | tf_op jit(solution)/shard_map/all_to_all | solution.py:297
  70.7 13.7 %collective-permute-start.2 = (bf16[2,896,128]{2,1,0:T(8,128)(2,1)S(1)}, bf16[2,896,128]{2,1,0:T(8,128)(2,1)}, u32[]{:S(2)}, u32[]{:S(2)}) collective-permute-start(bf16[2,896,128]{2,1,0:T(8,128)(2,1)S(1)} %shard_map.40.refs_0_), channel_id=1, source_target_pairs={{0,2},{1,15},{2,4},{3,1},{4,6},{5,3},{6,8},{7,5},{8,10},{9,7},{10,... | collective-permute-start | bytes 1376264 | tf_op jit(solution)/shard_map/ppermute | solution.py:234
  73.8 12.5 %collective-permute-start.3 = (bf16[2,896,128]{2,1,0:T(8,128)(2,1)S(1)}, bf16[2,896,128]{2,1,0:T(8,128)(2,1)}, u32[]{:S(2)}, u32[]{:S(2)}) collective-permute-start(bf16[2,896,128]{2,1,0:T(8,128)(2,1)S(1)} %collective-permute-done.1.after_ref.refs_2_), channel_id=1, source_target_pairs={{0,2},{1,15},{2,4},{3,1},{4,6},{5,3},{6,8},{7,5},{8,10},{9,7},{10,... | collective-permute-start | bytes 1376264 | tf_op jit(solution)/shard_map/ppermute | solution.py:234
  79.3 17.4 %collective-permute-start.7 = (bf16[2,896,128]{2,1,0:T(8,128)(2,1)S(1)}, bf16[2,896,128]{2,1,0:T(8,128)(2,1)S(1)}, u32[]{:S(2)}, u32[]{:S(2)}) collective-permute-start(bf16[2,896,128]{2,1,0:T(8,128)(2,1)S(1)} %collective-permute-done.1.after_ref.refs_2_), channel_id=1, source_target_pairs={{0,4},{1,13},{2,6},{3,15},{4,8},{5,1},{6,10},{7,3},{8,12},{9,5},{1... | collective-permute-start | bytes 1376264 | tf_op jit(solution)/shard_map/ppermute | solution.py:234
  81.3 15.4 %collective-permute-start.4 = (bf16[2,896,128]{2,1,0:T(8,128)(2,1)S(1)}, bf16[2,896,128]{2,1,0:T(8,128)(2,1)S(1)}, u32[]{:S(2)}, u32[]{:S(2)}) collective-permute-start(bf16[2,896,128]{2,1,0:T(8,128)(2,1)S(1)} %collective-permute-done.1.after_ref.refs_2_), channel_id=1, source_target_pairs={{0,1},{1,0},{2,3},{3,2},{4,5},{5,4},{6,7},{7,6},{8,9},{9,8},{10,11... | collective-permute-start | bytes 1376264 | tf_op jit(solution)/shard_map/ppermute | solution.py:238
  84.4 12.1 %collective-permute-start.5 = (bf16[2,896,128]{2,1,0:T(8,128)(2,1)}, bf16[2,896,128]{2,1,0:T(8,128)(2,1)S(1)}, u32[]{:S(2)}, u32[]{:S(2)}) collective-permute-start(bf16[2,896,128]{2,1,0:T(8,128)(2,1)} %collective-permute-done.2.refs_1_), channel_id=1, source_target_pairs={{0,1},{1,0},{2,3},{3,2},{4,5},{5,4},{6,7},{7,6},{8,9},{9,8},{10,11... | collective-permute-start | bytes 1376264 | tf_op jit(solution)/shard_map/ppermute | solution.py:238
  86.3 10.4 %collective-permute-start.6 = (bf16[2,896,128]{2,1,0:T(8,128)(2,1)}, bf16[2,896,128]{2,1,0:T(8,128)(2,1)S(1)}, u32[]{:S(2)}, u32[]{:S(2)}) collective-permute-start(bf16[2,896,128]{2,1,0:T(8,128)(2,1)} %collective-permute-done.3.refs_3_), channel_id=1, source_target_pairs={{0,1},{1,0},{2,3},{3,2},{4,5},{5,4},{6,7},{7,6},{8,9},{9,8},{10,11... | collective-permute-start | bytes 1376264 | tf_op jit(solution)/shard_map/ppermute | solution.py:238
  94.2 1.7 %copy-start = (bf16[4608,256]{1,0:T(8,128)(2,1)S(1)}, bf16[4608,256]{1,0:T(8,128)(2,1)}, u32[]{:S(2)}) copy-start(bf16[4608,256]{1,0:T(8,128)(2,1)} %shard_map.43.early_ref) | copy-start | bytes 7077892
